TPU v7x, 768 devices: a whole 4x8x12 slice. The times are simulated.
768 devices in a mesh: wide: 32 (over z_hi, x, core), narrow: 24 (over y, z_lo).
Axes of the slice: x: 4, y: 8, z: 12 (z_hi: 4, z_lo: 3; z = z_hi * 3 + z_lo), core: 2. Of those that a mesh axis runs over, the one named last changes fastest.
Arguments:
- picture_vectors: bfloat16 [24576, 1152], P('wide')
- sentence_vectors: bfloat16 [24576, 1152], P('wide')
- matched_text_indices: int32 [24576], P('wide'), may hold values from 0 to 24575, as said below
- partner_table: int32 [5, 32], replicated, may hold values from 0 to 31, as said below
- trained_steepness: float32 [1], replicated, may hold values from 60 to 120
- learned_shift: float32 [1], replicated, may hold values from -6 to -3
Outputs:
- photo_slopes: float32 [24576, 1152], P(('wide', 'narrow'))
- wording_slopes: float32 [24576, 1152], P(('wide', 'narrow'))
Inputs may be any that keep to these rules, and one draw needn't show every extreme that they name: `matched_text_indices`: every image's matching text lies in the image's own block of 768 consecutive rows, and every text is matched by exactly one image. Each row r is a perfect matching of the blocks of the form partner_table[r, i] = i XOR m_r, with round masks m_r that differ between rounds and are never 0.
All inputs are finite; a program needn't handle non-finite values.
Results may differ from a plain program's by a relative error of at most 0.0018.
Values may be sent and summed in bfloat16 or wider, within the bound.
No kernel may reach another device: no remote copies, remote signals or barrier semaphores. Data moves between devices by JAX's collectives and lax.ppermute only.
A program may use at most 64 MiB of HBM per device.

v0:
```python
import functools
import jax
import jax.numpy as jnp
from jax import lax
from jax.experimental import pallas as pl
from jax.experimental.pallas import tpu as pltpu
from jax.sharding import PartitionSpec as P

WIDE = 32
Z_SETS = [[low + 8 * z for z in range(4)] for low in range(8)]
VMEM_LIMIT = 48 * 1024 * 1024


def xor_pairs(mask):
    return [(i, i ^ mask) for i in range(WIDE)]


CAP = 2


def splits(rounds):
    sizes = range(CAP + 1)
    return [(a, b, c) for a in sizes for b in sizes for c in sizes if a + b + c <= rounds]


def move_along_x(counts, rounds, stack):
    tall = stack.shape[0] // rounds
    start = rounds - sum(counts)
    pieces = [stack[: start * tall]] if start else []
    spans = {}
    for mask, count in enumerate(counts, 1):
        spans[mask] = (start, count)
        start += count
    moved = {}
    for mask in (2, 1, 3):
        begin, count = spans[mask]
        if count:
            piece = stack[begin * tall : (begin + count) * tall]
            moved[mask] = lax.ppermute(piece, "wide", xor_pairs(2 * mask))
    pieces += [moved[mask] for mask in sorted(moved)]
    return jnp.concatenate(pieces, axis=0) if len(pieces) > 1 else pieces[0]


def move_spare(mask, count, rounds, stack):
    cut = stack.shape[0] // rounds * count
    moved = lax.ppermute(stack[:cut], "wide", xor_pairs(2 * mask))
    return jnp.concatenate([moved, stack[cut:]], axis=0) if count < rounds else moved


def exchange_x(rounds, main, spare, stack):
    stack = lax.switch(main, [functools.partial(move_along_x, c, rounds) for c in splits(rounds)], stack)
    moves = [lambda x: x]
    for mask in (1, 2, 3):
        for count in range(1, rounds - CAP + 1):
            moves.append(functools.partial(move_spare, mask, count, rounds))
    return lax.switch(spare, moves, stack)


def pick_kernel(rounds, table, *refs):
    shares, (stack, info) = refs[:4], refs[4:]
    my_z = lax.axis_index("wide") // 8
    masks = [table[r, 0] for r in range(rounds)]
    x_masks = [(mask >> 1) & 3 for mask in masks]
    keys = []
    for r in range(rounds):
        before = sum([(x_masks[s] == x_masks[r]).astype(jnp.int32) for s in range(r)], jnp.int32(0))
        spare = (x_masks[r] > 0) & (before >= CAP)
        keys.append(jnp.where(spare, 0, 1 + x_masks[r]))
    counts = [sum((x == k).astype(jnp.int32) for x in x_masks) for k in (1, 2, 3)]
    kept = [jnp.minimum(count, CAP) for count in counts]
    main = jnp.int32(0)
    for index, pattern in enumerate(splits(rounds)):
        hit = (kept[0] == pattern[0]) & (kept[1] == pattern[1]) & (kept[2] == pattern[2])
        main += jnp.where(hit, index, 0)
    spare = jnp.int32(0)
    for k in range(3):
        over = counts[k] - kept[k]
        spare += jnp.where(over > 0, k * (rounds - CAP) + over, 0)
    info[0] = main
    info[1] = spare
    tall = shares[0].shape[0]
    for place in range(rounds):
        mask = jnp.int32(0)
        for r in range(rounds):
            rank = jnp.int32(0)
            for s in range(rounds):
                if s != r:
                    ahead = keys[s] <= keys[r] if s < r else keys[s] < keys[r]
                    rank += ahead.astype(jnp.int32)
            mask += jnp.where(rank == place, masks[r], 0)
        z_mask = (mask >> 3) & 3
        info[2 + place] = mask & 1
        info[2 + rounds + place] = my_z ^ z_mask
        for z in range(4):

            @pl.when(z_mask == z)
            def _():
                stack[place * tall : (place + 1) * tall, :] = shares[z][...]


def dot_last(left, right):
    return lax.dot_general(left, right, (((1,), (1,)), ((), ())), preferred_element_type=jnp.float32)


def dot(left, right):
    return jnp.dot(left, right, preferred_element_type=jnp.float32)


def own_kernel(steepness, shift, matched, shares, pictures, texts, own):
    rows, span = pictures.shape
    share = own.shape[0] // 2
    first = lax.axis_index("wide") * rows
    begin = lax.axis_index("narrow") * share
    scale = steepness[0] / span
    bias = shift[0]
    lanes = lax.broadcasted_iota(jnp.int32, (share, rows), 1)
    mine = begin + lax.broadcasted_iota(jnp.int32, (share, rows), 0)
    matches = jnp.broadcast_to(matched[...], (share, rows))
    my_match = jnp.sum(jnp.where(lanes == mine, matches, 0), axis=1, keepdims=True)
    for kind, block in enumerate([texts, pictures]):
        span_rows = slice(kind * share, (kind + 1) * share)
        same = (my_match == first + lanes) if kind == 0 else (matches == first + mine)
        signs = jnp.where(same, 1.0, -1.0).astype(jnp.float32)
        logits = scale * dot_last(shares[span_rows, :], block[...]) + bias
        weights = (-scale * signs * jax.nn.sigmoid(-signs * logits)).astype(jnp.bfloat16)
        own[span_rows, :] = dot(weights, block[...])


def grad_kernel(rounds, info, steepness, shift, stack, pictures, texts, other_pictures, other_texts, back):
    span = pictures.shape[1]
    share = stack.shape[0] // rounds // 2
    scale = steepness[0] / span
    bias = shift[0]
    for kind, (block, other) in enumerate([(texts, other_texts), (pictures, other_pictures)]):
        left = jnp.concatenate(
            [stack[(2 * place + kind) * share : (2 * place + kind + 1) * share, :] for place in range(rounds)],
            axis=0,
        )
        near = dot_last(left, block[...])
        far = dot_last(left, other[...])
        near_weights = []
        far_weights = []
        for place in range(rounds):
            apart = info[2 + place] == 1
            span_rows = slice(place * share, (place + 1) * share)
            products = jnp.where(apart, far[span_rows], near[span_rows])
            weights = scale * jax.nn.sigmoid(scale * products + bias)
            near_weights.append(jnp.where(apart, 0.0, weights).astype(jnp.bfloat16))
            far_weights.append(jnp.where(apart, weights, 0.0).astype(jnp.bfloat16))
        slopes = dot(jnp.concatenate(near_weights, axis=0), block[...]) + dot(
            jnp.concatenate(far_weights, axis=0), other[...]
        )
        for place in range(rounds):
            back[(2 * place + kind) * share : (2 * place + kind + 1) * share, :] = slopes[
                place * share : (place + 1) * share
            ]


def local(
    picture_vectors,
    sentence_vectors,
    matched_text_indices,
    partner_table,
    trained_steepness,
    learned_shift,
):
    rows, span = picture_vectors.shape
    rounds = partner_table.shape[0]
    share = rows // lax.axis_size("narrow")
    begin = lax.axis_index("narrow") * share
    smem = pl.BlockSpec(memory_space=pltpu.SMEM)
    vmem = pl.BlockSpec(memory_space=pltpu.VMEM)

    other_pictures = lax.ppermute(picture_vectors, "wide", xor_pairs(1))
    other_texts = lax.ppermute(sentence_vectors, "wide", xor_pairs(1))
    shares = jnp.concatenate(
        [
            lax.dynamic_slice_in_dim(picture_vectors, begin, share, 0),
            lax.dynamic_slice_in_dim(sentence_vectors, begin, share, 0),
        ],
        axis=0,
    )
    by_z = [shares] + [lax.ppermute(shares, "wide", xor_pairs(8 * mask)) for mask in (1, 2, 3)]
    own = pl.pallas_call(
        own_kernel,
        out_shape=jax.ShapeDtypeStruct((2 * share, span), jnp.float32),
        in_specs=[smem, smem, vmem, vmem, vmem, vmem],
        out_specs=vmem,
        compiler_params=pltpu.CompilerParams(vmem_limit_bytes=VMEM_LIMIT),
    )(
        trained_steepness,
        learned_shift,
        matched_text_indices[None, :],
        shares,
        picture_vectors,
        sentence_vectors,
    )
    stack, info = pl.pallas_call(
        functools.partial(pick_kernel, rounds),
        out_shape=[
            jax.ShapeDtypeStruct((rounds * 2 * share, span), jnp.bfloat16),
            jax.ShapeDtypeStruct((2 + 2 * rounds,), jnp.int32),
        ],
        in_specs=[smem] + [vmem] * 4,
        out_specs=[vmem, smem],
    )(partner_table, *by_z)
    stack = exchange_x(rounds, info[0], info[1], stack)
    back = pl.pallas_call(
        functools.partial(grad_kernel, rounds),
        out_shape=jax.ShapeDtypeStruct((rounds * 2 * share, span), jnp.float32),
        in_specs=[smem, smem, smem] + [vmem] * 5,
        out_specs=vmem,
        compiler_params=pltpu.CompilerParams(vmem_limit_bytes=VMEM_LIMIT),
    )(
        info,
        trained_steepness,
        learned_shift,
        stack,
        picture_vectors,
        sentence_vectors,
        other_pictures,
        other_texts,
    )
    back = exchange_x(rounds, info[0], info[1], back.astype(jnp.float16))

    back = back.reshape(rounds, 2 * share, span).astype(jnp.float32)
    homes = info[2 + rounds :]
    sums = jnp.stack(
        [
            jnp.sum(jnp.where((homes == z)[:, None, None], back, 0.0), axis=0).astype(jnp.float16)
            for z in range(4)
        ],
        axis=0,
    )
    arrived = lax.all_to_all(sums, "wide", 0, 0, axis_index_groups=Z_SETS)
    slopes = own + jnp.sum(arrived.astype(jnp.float32), axis=0)
    return slopes[:share], slopes[share:]


def solution(mesh):
    in_specs = (P("wide", None), P("wide", None), P("wide"), P(), P(), P())
    out_specs = (P(("wide", "narrow"), None), P(("wide", "narrow"), None))
    return jax.shard_map(local, mesh=mesh, in_specs=in_specs, out_specs=out_specs, check_vma=False)
```

profile of v0, /device:TPU:129, one launch (start us, length us, event | category | flops | bytes accessed | tf_op | source)
XLA Modules:
  0.0 150.7 jit_solution(10540055784484407873)
XLA Ops:
  0.6 2.6 %collective-permute-start.123 = (bf16[768,1152]{1,0:T(8,128)(2,1)}, bf16[768,1152]{1,0:T(8,128)(2,1)}, u32[]{:S(2)}, u32[]{:S(2)}) collective-permute-start(bf16[768,1152]{1,0:T(8,128)(2,1)} %pictures.3), channel_id=1, source_target_pairs={{0,24},{24,0},{48,72},{72,48},{96,120},{120,96},{144,168},{168,144... | collective-permute-start | bytes 5308424 | tf_op jit(solution)/shard_map/ppermute | solution.py:174
  3.2 1.9 %collective-permute-start.124 = (bf16[768,1152]{1,0:T(8,128)(2,1)}, bf16[768,1152]{1,0:T(8,128)(2,1)}, u32[]{:S(2)}, u32[]{:S(2)}) collective-permute-start(bf16[768,1152]{1,0:T(8,128)(2,1)} %texts.3), channel_id=1, source_target_pairs={{0,24},{24,0},{48,72},{72,48},{96,120},{120,96},{144,168},{168,144... | collective-permute-start | bytes 5308424 | tf_op jit(solution)/shard_map/ppermute | solution.py:175
  5.2 0.9 constant_dynamic-slice_fusion
  6.1 0.9 constant_dynamic-slice_fusion.1
  7.0 0.0 copy-start.2
  7.0 8.8 %collective-permute-start.120 = (bf16[64,1152]{1,0:T(8,128)(2,1)S(1)}, bf16[64,1152]{1,0:T(8,128)(2,1)S(1)}, u32[]{:S(2)}, u32[]{:S(2)}) collective-permute-start(bf16[64,1152]{1,0:T(8,128)(2,1)S(1)} %pad_maximum_fusion.69.shares.refs_0_), channel_id=1, source_target_pairs={{0,192},{24,216},{48,240},{72,264},{96,288},{120,312},{144,336},{1... | collective-permute-start | bytes 442376 | tf_op jit(solution)/shard_map/ppermute | solution.py:183
  15.8 8.5 %collective-permute-start.121 = (bf16[64,1152]{1,0:T(8,128)(2,1)S(1)}, bf16[64,1152]{1,0:T(8,128)(2,1)S(1)}, u32[]{:S(2)}, u32[]{:S(2)}) collective-permute-start(bf16[64,1152]{1,0:T(8,128)(2,1)S(1)} %pad_maximum_fusion.69.shares.refs_0_), channel_id=1, source_target_pairs={{0,384},{24,408},{48,432},{72,456},{96,480},{120,504},{144,528},{1... | collective-permute-start | bytes 442376 | tf_op jit(solution)/shard_map/ppermute | solution.py:183
  24.4 1.9 %collective-permute-start.122 = (bf16[64,1152]{1,0:T(8,128)(2,1)S(1)}, bf16[64,1152]{1,0:T(8,128)(2,1)S(1)}, u32[]{:S(2)}, u32[]{:S(2)}) collective-permute-start(bf16[64,1152]{1,0:T(8,128)(2,1)S(1)} %pad_maximum_fusion.69.shares.refs_0_), channel_id=1, source_target_pairs={{0,576},{24,600},{48,624},{72,648},{96,672},{120,696},{144,720},{1... | collective-permute-start | bytes 442376 | tf_op jit(solution)/shard_map/ppermute | solution.py:183
  27.6 3.4 %collective-permute-done.120.refs_1_ = bf16[64,1152]{1,0:T(8,128)(2,1)S(1)} collective-permute-done((bf16[64,1152]{1,0:T(8,128)(2,1)S(1)}, bf16[64,1152]{1,0:T(8,128)(2,1)S(1)}, u32[]{:S(2)}, u32[]{:S(2)}) %collective-permute-start.120) | collective-permute-done | bytes 147488 | tf_op jit(solution)/shard_map/ppermute | solution.py:183
  31.0 10.5 %collective-permute-done.121.refs_2_ = bf16[64,1152]{1,0:T(8,128)(2,1)S(1)} collective-permute-done((bf16[64,1152]{1,0:T(8,128)(2,1)S(1)}, bf16[64,1152]{1,0:T(8,128)(2,1)S(1)}, u32[]{:S(2)}, u32[]{:S(2)}) %collective-permute-start.121) | collective-permute-done | bytes 147488 | tf_op jit(solution)/shard_map/ppermute | solution.py:183
  41.5 0.0 collective-permute-done.122.refs_3_
  41.5 0.0 copy-done.2
  41.5 0.0 copy-done.7
  41.5 0.6 copy-done.8
  42.1 0.7 copy-done.9
  42.8 1.9 %shard_map.78 = (bf16[320,1152]{1,0:T(8,128)(2,1)S(1)}, s32[12]{0:T(128)}) custom-call(s32[5,32]{1,0:T(8,128)} %table.1, bf16[64,1152]{1,0:T(8,128)(2,1)} %copy-done.2, bf16[64,1152]{1,0:T(8,128)(2,1)} %copy-done.7, bf16[64,1152]{1,0:T(8,128)(2,1)} %copy-done.8, bf16[64,1152]{1,0:T(8,128)(2,1)} %copy-done.9), custom_call_target="tpu_custom_call" | custom-call | tf_op jit(solution)/shard_map/pallas_call | solution.py:198
  44.7 1.3 fusion.43
  46.7 15.7 %conditional.4 = (bf16[320,1152]{1,0:T(8,128)(2,1)S(1)}) conditional(s32[]{:T(128)} %bitcast.1, bf16[320,1152]{1,0:T(8,128)(2,1)S(1)} %get-tuple-element.159, bf16[320,1152]{1,0:T(8,128)(2,1)S(1)} %get-tuple-element.159, bf16[320,1152]{1,0:T(8,128)(2,1)S(1)} %get-tuple-element.159, ...), branch_computations={%region_0.0_spmd, %region_1.0_spmd, %region_2.0_spmd, %region_3.0_... | conditional | flops 2949120 | bytes 5898368 | solution.py:51
  46.8 4.6 %collective-permute-start.34 = (bf16[128,1152]{1,0:T(8,128)(2,1)S(1)}, bf16[128,1152]{1,0:T(8,128)(2,1)S(1)}, u32[]{:S(2)}, u32[]{:S(2)}) collective-permute-start(bf16[128,1152]{1,0:T(8,128)(2,1)S(1)} %get-tuple-element.169), channel_id=1, source_target_pairs={{0,96},{24,120},{48,144},{72,168},{96,0},{120,24},{144,48},{168,72... | collective-permute-start | bytes 884744 | tf_op jit(solution)/shard_map/cond/branch_7_fun/ppermute | solution.py:39
  51.4 2.8 %collective-permute-start.35 = (bf16[64,1152]{1,0:T(8,128)(2,1)S(1)}, bf16[64,1152]{1,0:T(8,128)(2,1)S(1)}, u32[]{:S(2)}, u32[]{:S(2)}) collective-permute-start(bf16[64,1152]{1,0:T(8,128)(2,1)S(1)} %slice.392), channel_id=1, source_target_pairs={{0,144},{24,168},{48,96},{72,120},{96,48},{120,72},{144,0},{168,24... | collective-permute-start | bytes 442376 | tf_op jit(solution)/shard_map/cond/branch_7_fun/ppermute | solution.py:39
  54.2 8.1 %collective-permute-done.35 = bf16[64,1152]{1,0:T(8,128)(2,1)S(1)} collective-permute-done((bf16[64,1152]{1,0:T(8,128)(2,1)S(1)}, bf16[64,1152]{1,0:T(8,128)(2,1)S(1)}, u32[]{:S(2)}, u32[]{:S(2)}) %collective-permute-start.35) | collective-permute-done | bytes 147488 | tf_op jit(solution)/shard_map/cond/branch_7_fun/ppermute | solution.py:39
  62.3 0.0 collective-permute-done.34
  62.3 0.1 pad_maximum_fusion.6
  62.4 0.0 copy-start.6
  62.9 0.3 copy-done.6
  63.3 10.4 %conditional.5 = (bf16[320,1152]{1,0:T(8,128)(2,1)}) conditional(s32[]{:T(128)} %bitcast, bf16[320,1152]{1,0:T(8,128)(2,1)} %copy-done.6, bf16[320,1152]{1,0:T(8,128)(2,1)} %copy-done.6, bf16[320,1152]{1,0:T(8,128)(2,1)} %copy-done.6, bf16[320,1152]{1,0:T(8,128)(2,1)} %copy-done.6, ...), branch_computations={%region_26.0_spmd, %region_27.0_spmd, %region_28.0_spmd, %region_2... | conditional | flops 1474560 | bytes 4718640 | solution.py:56
  63.3 1.1 slice.455
  64.3 4.7 %collective-permute-start.9 = (bf16[64,1152]{1,0:T(8,128)(2,1)S(1)}, bf16[64,1152]{1,0:T(8,128)(2,1)S(1)}, u32[]{:S(2)}, u32[]{:S(2)}) collective-permute-start(bf16[64,1152]{1,0:T(8,128)(2,1)S(1)} %slice.455), channel_id=1, source_target_pairs={{0,96},{24,120},{48,144},{72,168},{96,0},{120,24},{144,48},{168,72... | collective-permute-start | bytes 442376 | tf_op jit(solution)/shard_map/cond/branch_4_fun/ppermute | solution.py:46
  69.0 1.1 slice.456
  70.2 2.6 %collective-permute-done.9 = bf16[64,1152]{1,0:T(8,128)(2,1)S(1)} collective-permute-done((bf16[64,1152]{1,0:T(8,128)(2,1)S(1)}, bf16[64,1152]{1,0:T(8,128)(2,1)S(1)}, u32[]{:S(2)}, u32[]{:S(2)}) %collective-permute-start.9) | collective-permute-done | bytes 147488 | tf_op jit(solution)/shard_map/cond/branch_4_fun/ppermute | solution.py:46
  72.8 0.9 pad_maximum_fusion.28
  73.7 0.0 copy-done.5
  73.7 0.7 broadcast_compare_fusion
  74.4 0.0 collective-permute-done.123.other_pictures
  74.4 0.0 collective-permute-done.124.other_texts
  74.4 6.1 %shard_map.79 = f32[320,1152]{1,0:T(8,128)S(1)} custom-call(s32[12]{0:T(128)S(1)} %copy-done.5, f32[1]{0:T(128)S(6)} %copy.80.steepness, f32[1]{0:T(128)S(6)} %copy.81.shift, bf16[320,1152]{1,0:T(8,128)(2,1)} %get-tuple-element.261.stack, bf16[768,1152]{1,0:T(8,128)(2,1)S(1)} %copy-done.1, bf16[768,1152]{1,0:T(8,128)(2,1)S(1)} %copy-done, ...), custom_call_target="tpu_custom_call" | custom-call | tf_op jit(solution)/shard_map/pallas_call | solution.py:208
  80.5 0.9 convert_element_type.164
  81.5 16.7 %conditional.6 = (f16[320,1152]{1,0:T(8,128)(2,1)}) conditional(s32[]{:T(128)} %bitcast.1, f16[320,1152]{1,0:T(8,128)(2,1)} %convert_element_type.164, f16[320,1152]{1,0:T(8,128)(2,1)} %convert_element_type.164, f16[320,1152]{1,0:T(8,128)(2,1)} %convert_element_type.164, ...), branch_computations={%region_36.0_spmd, %region_37.0_spmd, %region_38.0_spmd, %region_3... | conditional | flops 1105920 | bytes 5898368 | solution.py:51
  81.5 1.2 fusion.25
  82.6 4.6 %collective-permute-start.79 = (f16[128,1152]{1,0:T(8,128)(2,1)S(1)}, f16[128,1152]{1,0:T(8,128)(2,1)S(1)}, u32[]{:S(2)}, u32[]{:S(2)}) collective-permute-start(f16[128,1152]{1,0:T(8,128)(2,1)S(1)} %get-tuple-element.211), channel_id=1, source_target_pairs={{0,96},{24,120},{48,144},{72,168},{96,0},{120,24},{144,48},{168,72... | collective-permute-start | bytes 884744 | tf_op jit(solution)/shard_map/cond/branch_7_fun/ppermute | solution.py:39
  87.2 0.9 slice.483
  88.2 2.8 %collective-permute-start.80 = (f16[64,1152]{1,0:T(8,128)(2,1)S(1)}, f16[64,1152]{1,0:T(8,128)(2,1)S(1)}, u32[]{:S(2)}, u32[]{:S(2)}) collective-permute-start(f16[64,1152]{1,0:T(8,128)(2,1)S(1)} %slice.483), channel_id=1, source_target_pairs={{0,144},{24,168},{48,96},{72,120},{96,48},{120,72},{144,0},{168,24... | collective-permute-start | bytes 442376 | tf_op jit(solution)/shard_map/cond/branch_7_fun/ppermute | solution.py:39
  90.9 6.2 %collective-permute-done.80 = f16[64,1152]{1,0:T(8,128)(2,1)S(1)} collective-permute-done((f16[64,1152]{1,0:T(8,128)(2,1)S(1)}, f16[64,1152]{1,0:T(8,128)(2,1)S(1)}, u32[]{:S(2)}, u32[]{:S(2)}) %collective-permute-start.80) | collective-permute-done | bytes 147488 | tf_op jit(solution)/shard_map/cond/branch_7_fun/ppermute | solution.py:39
  97.1 0.0 collective-permute-done.79
  97.1 1.1 pad_maximum_fusion.40
  98.2 10.7 %conditional.7 = (f16[320,1152]{1,0:T(8,128)(2,1)}) conditional(s32[]{:T(128)} %bitcast, f16[320,1152]{1,0:T(8,128)(2,1)} %get-tuple-element.262, f16[320,1152]{1,0:T(8,128)(2,1)} %get-tuple-element.262, f16[320,1152]{1,0:T(8,128)(2,1)} %get-tuple-element.262, f16[320,1152]{1,0:T(8,128)(2,1)} %get-tuple-element.262, ...), branch_computations={%region_62.0_spmd, %region_63.0_spmd, %region_64.0_spmd, %region_6... | conditional | flops 368640 | bytes 4718640 | solution.py:56
  98.2 0.9 slice.546
  99.1 5.6 %collective-permute-start.24 = (f16[64,1152]{1,0:T(8,128)(2,1)S(1)}, f16[64,1152]{1,0:T(8,128)(2,1)S(1)}, u32[]{:S(2)}, u32[]{:S(2)}) collective-permute-start(f16[64,1152]{1,0:T(8,128)(2,1)S(1)} %slice.546), channel_id=1, source_target_pairs={{0,96},{24,120},{48,144},{72,168},{96,0},{120,24},{144,48},{168,72... | collective-permute-start | bytes 442376 | tf_op jit(solution)/shard_map/cond/branch_4_fun/ppermute | solution.py:46
  104.7 1.2 slice.547
  105.9 2.0 %collective-permute-done.24 = f16[64,1152]{1,0:T(8,128)(2,1)S(1)} collective-permute-done((f16[64,1152]{1,0:T(8,128)(2,1)S(1)}, f16[64,1152]{1,0:T(8,128)(2,1)S(1)}, u32[]{:S(2)}, u32[]{:S(2)}) %collective-permute-start.24) | collective-permute-done | bytes 147488 | tf_op jit(solution)/shard_map/cond/branch_4_fun/ppermute | solution.py:46
  107.9 1.0 pad_maximum_fusion.62
  108.9 1.8 %fusion = (f32[64,1152]{1,0:T(8,128)S(1)}, f32[64,1152]{1,0:T(8,128)S(1)}, f32[64,1152]{1,0:T(8,128)S(1)}, f32[64,1152]{1,0:T(8,128)S(1)}) fusion(f16[5,64,1152]{2,1,0:T(8,128)(2,1)} %bitcast.12, pred[5]{0:T(512)(128)(4,1)S(1)} %copy-done.11, pred[5]{0:T(512)(128)(4,1)S(1)} %get-tuple-element.251, pred[5]{0:T(512)(128)(4,1)S(1)} %get-tuple-element.252, ...), kind=kLoop, calls=%fused_computation.72 | loop fusion | flops 3022848 | bytes 1916948 | tf_op jit(solution)/shard_map/reduce_sum | solution.py:230
  110.8 0.0 copy-start.10
  110.8 1.0 pad_maximum_fusion.68
  111.8 10.7 %all-to-all-start = ((f16[4,64,1152]{2,1,0:T(8,128)(2,1)}), f16[4,64,1152]{2,1,0:T(8,128)(2,1)}, u32[]{:S(2)}, u32[]{:S(2)}) async-start(f16[4,64,1152]{2,1,0:T(8,128)(2,1)} %pad_maximum_fusion.68), calls=%async_computation | async-start | bytes 1179648 | tf_op jit(solution)/shard_map/all_to_all | solution.py:235
  122.5 0.0 copy-start.3
  122.5 0.9 copy-done.3
  123.4 2.2 %shard_map.77 = f32[64,1152]{1,0:T(8,128)S(1)} custom-call(f32[1]{0:T(128)S(6)} %copy.80.steepness, f32[1]{0:T(128)S(6)} %copy.81.shift, s32[1,768]{1,0:T(1,128)S(1)} %broadcast_in_dim.37.matched, bf16[64,1152]{1,0:T(8,128)(2,1)S(1)} %copy-done.3, bf16[768,1152]{1,0:T(8,128)(2,1)S(1)} %copy-done.1, bf16[768,1152]{1,0:T(8,128)(2,1)S(1)} %copy-done), custom_call_target="tpu_custom_call" | custom-call | tf_op jit(solution)/shard_map/pallas_call | solution.py:184
  125.6 0.0 copy-start.4
  125.7 0.7 copy-done.4
  126.4 21.4 %all-to-all-done = f16[4,64,1152]{2,1,0:T(8,128)(2,1)} async-done(((f16[4,64,1152]{2,1,0:T(8,128)(2,1)}), f16[4,64,1152]{2,1,0:T(8,128)(2,1)}, u32[]{:S(2)}, u32[]{:S(2)}) %all-to-all-start) | async-done | bytes 589856 | tf_op jit(solution)/shard_map/all_to_all | solution.py:235
  147.8 1.2 convert_reduce_fusion
  148.9 1.0 add.8
  149.9 0.7 fusion.42
  (17 shorter events, 0.2 us)
Async XLA Ops:
  0.6 73.7 %collective-permute-start.123 = (bf16[768,1152]{1,0:T(8,128)(2,1)}, bf16[768,1152]{1,0:T(8,128)(2,1)}, u32[]{:S(2)}, u32[]{:S(2)}) collective-permute-start(bf16[768,1152]{1,0:T(8,128)(2,1)} %pictures.3), channel_id=1, source_target_pairs={{0,24},{24,0},{48,72},{72,48},{96,120},{120,96},{144,168},{168,144... | collective-permute-start | bytes 5308424 | tf_op jit(solution)/shard_map/ppermute | solution.py:174
  3.2 71.1 %collective-permute-start.124 = (bf16[768,1152]{1,0:T(8,128)(2,1)}, bf16[768,1152]{1,0:T(8,128)(2,1)}, u32[]{:S(2)}, u32[]{:S(2)}) collective-permute-start(bf16[768,1152]{1,0:T(8,128)(2,1)} %texts.3), channel_id=1, source_target_pairs={{0,24},{24,0},{48,72},{72,48},{96,120},{120,96},{144,168},{168,144... | collective-permute-start | bytes 5308424 | tf_op jit(solution)/shard_map/ppermute | solution.py:175
  7.0 34.5 %copy-start.2 = (bf16[64,1152]{1,0:T(8,128)(2,1)}, bf16[64,1152]{1,0:T(8,128)(2,1)S(1)}, u32[]{:S(2)}) copy-start(bf16[64,1152]{1,0:T(8,128)(2,1)S(1)} %pad_maximum_fusion.69.shares.refs_0_) | copy-start | bytes 442372
  7.0 24.0 %collective-permute-start.120 = (bf16[64,1152]{1,0:T(8,128)(2,1)S(1)}, bf16[64,1152]{1,0:T(8,128)(2,1)S(1)}, u32[]{:S(2)}, u32[]{:S(2)}) collective-permute-start(bf16[64,1152]{1,0:T(8,128)(2,1)S(1)} %pad_maximum_fusion.69.shares.refs_0_), channel_id=1, source_target_pairs={{0,192},{24,216},{48,240},{72,264},{96,288},{120,312},{144,336},{1... | collective-permute-start | bytes 442376 | tf_op jit(solution)/shard_map/ppermute | solution.py:183
  15.8 25.7 %collective-permute-start.121 = (bf16[64,1152]{1,0:T(8,128)(2,1)S(1)}, bf16[64,1152]{1,0:T(8,128)(2,1)S(1)}, u32[]{:S(2)}, u32[]{:S(2)}) collective-permute-start(bf16[64,1152]{1,0:T(8,128)(2,1)S(1)} %pad_maximum_fusion.69.shares.refs_0_), channel_id=1, source_target_pairs={{0,384},{24,408},{48,432},{72,456},{96,480},{120,504},{144,528},{1... | collective-permute-start | bytes 442376 | tf_op jit(solution)/shard_map/ppermute | solution.py:183
  24.4 17.1 %collective-permute-start.122 = (bf16[64,1152]{1,0:T(8,128)(2,1)S(1)}, bf16[64,1152]{1,0:T(8,128)(2,1)S(1)}, u32[]{:S(2)}, u32[]{:S(2)}) collective-permute-start(bf16[64,1152]{1,0:T(8,128)(2,1)S(1)} %pad_maximum_fusion.69.shares.refs_0_), channel_id=1, source_target_pairs={{0,576},{24,600},{48,624},{72,648},{96,672},{120,696},{144,720},{1... | collective-permute-start | bytes 442376 | tf_op jit(solution)/shard_map/ppermute | solution.py:183
  31.0 10.5 %copy-start.7 = (bf16[64,1152]{1,0:T(8,128)(2,1)}, bf16[64,1152]{1,0:T(8,128)(2,1)S(1)}, u32[]{:S(2)}) copy-start(bf16[64,1152]{1,0:T(8,128)(2,1)S(1)} %collective-permute-done.120.refs_1_) | copy-start | bytes 442372
  41.5 0.7 copy-start.8
  42.1 0.7 copy-start.9
  46.8 15.5 %collective-permute-start.34 = (bf16[128,1152]{1,0:T(8,128)(2,1)S(1)}, bf16[128,1152]{1,0:T(8,128)(2,1)S(1)}, u32[]{:S(2)}, u32[]{:S(2)}) collective-permute-start(bf16[128,1152]{1,0:T(8,128)(2,1)S(1)} %get-tuple-element.169), channel_id=1, source_target_pairs={{0,96},{24,120},{48,144},{72,168},{96,0},{120,24},{144,48},{168,72... | collective-permute-start | bytes 884744 | tf_op jit(solution)/shard_map/cond/branch_7_fun/ppermute | solution.py:39
  51.4 10.9 %collective-permute-start.35 = (bf16[64,1152]{1,0:T(8,128)(2,1)S(1)}, bf16[64,1152]{1,0:T(8,128)(2,1)S(1)}, u32[]{:S(2)}, u32[]{:S(2)}) collective-permute-start(bf16[64,1152]{1,0:T(8,128)(2,1)S(1)} %slice.392), channel_id=1, source_target_pairs={{0,144},{24,168},{48,96},{72,120},{96,48},{120,72},{144,0},{168,24... | collective-permute-start | bytes 442376 | tf_op jit(solution)/shard_map/cond/branch_7_fun/ppermute | solution.py:39
  62.4 0.9 copy-start.6
  63.2 10.5 %copy-start.5 = (s32[12]{0:T(128)S(1)}, s32[12]{0:T(128)}, u32[]{:S(2)}) copy-start(s32[12]{0:T(128)} %get-tuple-element.158.info) | copy-start | bytes 148
  63.2 11.1 %copy-start = (bf16[768,1152]{1,0:T(8,128)(2,1)S(1)}, bf16[768,1152]{1,0:T(8,128)(2,1)}, u32[]{:S(2)}) copy-start(bf16[768,1152]{1,0:T(8,128)(2,1)} %texts.3) | copy-start | bytes 5308420
  63.3 11.1 %copy-start.1 = (bf16[768,1152]{1,0:T(8,128)(2,1)S(1)}, bf16[768,1152]{1,0:T(8,128)(2,1)}, u32[]{:S(2)}) copy-start(bf16[768,1152]{1,0:T(8,128)(2,1)} %pictures.3) | copy-start | bytes 5308420
  64.3 8.4 %collective-permute-start.9 = (bf16[64,1152]{1,0:T(8,128)(2,1)S(1)}, bf16[64,1152]{1,0:T(8,128)(2,1)S(1)}, u32[]{:S(2)}, u32[]{:S(2)}) collective-permute-start(bf16[64,1152]{1,0:T(8,128)(2,1)S(1)} %slice.455), channel_id=1, source_target_pairs={{0,96},{24,120},{48,144},{72,168},{96,0},{120,24},{144,48},{168,72... | collective-permute-start | bytes 442376 | tf_op jit(solution)/shard_map/cond/branch_4_fun/ppermute | solution.py:46
  82.6 14.5 %collective-permute-start.79 = (f16[128,1152]{1,0:T(8,128)(2,1)S(1)}, f16[128,1152]{1,0:T(8,128)(2,1)S(1)}, u32[]{:S(2)}, u32[]{:S(2)}) collective-permute-start(f16[128,1152]{1,0:T(8,128)(2,1)S(1)} %get-tuple-element.211), channel_id=1, source_target_pairs={{0,96},{24,120},{48,144},{72,168},{96,0},{120,24},{144,48},{168,72... | collective-permute-start | bytes 884744 | tf_op jit(solution)/shard_map/cond/branch_7_fun/ppermute | solution.py:39
  88.2 9.0 %collective-permute-start.80 = (f16[64,1152]{1,0:T(8,128)(2,1)S(1)}, f16[64,1152]{1,0:T(8,128)(2,1)S(1)}, u32[]{:S(2)}, u32[]{:S(2)}) collective-permute-start(f16[64,1152]{1,0:T(8,128)(2,1)S(1)} %slice.483), channel_id=1, source_target_pairs={{0,144},{24,168},{48,96},{72,120},{96,48},{120,72},{144,0},{168,24... | collective-permute-start | bytes 442376 | tf_op jit(solution)/shard_map/cond/branch_7_fun/ppermute | solution.py:39
  98.2 10.7 %copy-start.11 = (pred[5]{0:T(512)(128)(4,1)S(1)}, pred[5]{0:T(512)(128)(4,1)}, u32[]{:S(2)}) copy-start(pred[5]{0:T(512)(128)(4,1)} %get-tuple-element.253) | copy-start | bytes 19
  99.1 8.7 %collective-permute-start.24 = (f16[64,1152]{1,0:T(8,128)(2,1)S(1)}, f16[64,1152]{1,0:T(8,128)(2,1)S(1)}, u32[]{:S(2)}, u32[]{:S(2)}) collective-permute-start(f16[64,1152]{1,0:T(8,128)(2,1)S(1)} %slice.546), channel_id=1, source_target_pairs={{0,96},{24,120},{48,144},{72,168},{96,0},{120,24},{144,48},{168,72... | collective-permute-start | bytes 442376 | tf_op jit(solution)/shard_map/cond/branch_4_fun/ppermute | solution.py:46
  110.8 11.8 %copy-start.10 = (s32[768]{0:T(1024)S(1)}, s32[768]{0:T(1024)}, u32[]{:S(2)}) copy-start(s32[768]{0:T(1024)} %param.80) | copy-start | bytes 9220
  111.8 35.9 %all-to-all-start = ((f16[4,64,1152]{2,1,0:T(8,128)(2,1)}), f16[4,64,1152]{2,1,0:T(8,128)(2,1)}, u32[]{:S(2)}, u32[]{:S(2)}) async-start(f16[4,64,1152]{2,1,0:T(8,128)(2,1)} %pad_maximum_fusion.68), calls=%async_computation | async-start | bytes 1179648 | tf_op jit(solution)/shard_map/all_to_all | solution.py:235
  122.5 0.9 copy-start.3
  125.6 0.7 copy-start.4
where the time goes:
time: 152 us; the launch traced here: 151 us
  starting transfers between devices  59.5 us (39%)
  waiting for transfers between devices  54.2 us (36%)
  local copies, waits for them, and re-layouts  13.5 us (9%)
  Pallas kernels  10.3 us (7%)
  other arithmetic  9.75 us (6%)
  between operations  3.32 us (2%)
    all_to_all x1, waiting for transfers between devices, local(): arrived = lax.all_to_all(sums, 'wide', 0, 0, axis_index_groups=Z_SETS)  21.4 us
    ppermute x3, starting transfers between devices, local(): lax.ppermute(shares, 'wide', xor_pairs(8 * mask))  19.3 us
    ppermute x4, starting transfers between devices, move_along_x(): moved[mask] = lax.ppermute(piece, 'wide', xor_pairs(2 * mask))  14.7 us
    ppermute x4, waiting for transfers between devices, move_along_x(): moved[mask] = lax.ppermute(piece, 'wide', xor_pairs(2 * mask))  14.3 us
    ppermute x3, waiting for transfers between devices, local(): lax.ppermute(shares, 'wide', xor_pairs(8 * mask))  13.9 us
    all_to_all x1, starting transfers between devices, local(): arrived = lax.all_to_all(sums, 'wide', 0, 0, axis_index_groups=Z_SETS)  10.7 us
    ppermute x2, starting transfers between devices, move_spare(): moved = lax.ppermute(stack[:cut], 'wide', xor_pairs(2 * mask))  10.3 us
    pallas_call x1, Pallas kernels, local(): pl.pallas_call(functools.partial(grad_kernel, rounds), out_shape=jax.Shap...  6.12 us
  transfers between devices with their start and end apart: 12, of which 7 were waited for; matrix products, arithmetic and copies ran while one was open for 6% of the time, Pallas kernels for 3%

commit v1 on v0

--- a/solution.py
+++ b/solution.py
@@ -8,7 +8,9 @@
 
 WIDE = 32
 Z_SETS = [[low + 8 * z for z in range(4)] for low in range(8)]
-VMEM_LIMIT = 48 * 1024 * 1024
+PICK_VMEM = 4 * 1024 * 1024
+OWN_VMEM = 12 * 1024 * 1024
+GRAD_VMEM = 24 * 1024 * 1024
 
 
 def xor_pairs(mask):
@@ -56,29 +58,27 @@
     return lax.switch(spare, moves, stack)
 
 
-def pick_kernel(rounds, table, *refs):
-    shares, (stack, info) = refs[:4], refs[4:]
+def order_kernel(rounds, table, main, spare, info):
     my_z = lax.axis_index("wide") // 8
     masks = [table[r, 0] for r in range(rounds)]
     x_masks = [(mask >> 1) & 3 for mask in masks]
     keys = []
     for r in range(rounds):
         before = sum([(x_masks[s] == x_masks[r]).astype(jnp.int32) for s in range(r)], jnp.int32(0))
-        spare = (x_masks[r] > 0) & (before >= CAP)
-        keys.append(jnp.where(spare, 0, 1 + x_masks[r]))
+        beyond = (x_masks[r] > 0) & (before >= CAP)
+        keys.append(jnp.where(beyond, 0, 1 + x_masks[r]))
     counts = [sum((x == k).astype(jnp.int32) for x in x_masks) for k in (1, 2, 3)]
     kept = [jnp.minimum(count, CAP) for count in counts]
-    main = jnp.int32(0)
-    for index, pattern in enumerate(splits(rounds)):
+    index = jnp.int32(0)
+    for place, pattern in enumerate(splits(rounds)):
         hit = (kept[0] == pattern[0]) & (kept[1] == pattern[1]) & (kept[2] == pattern[2])
-        main += jnp.where(hit, index, 0)
-    spare = jnp.int32(0)
+        index += jnp.where(hit, place, 0)
+    main[0] = index
+    index = jnp.int32(0)
     for k in range(3):
         over = counts[k] - kept[k]
-        spare += jnp.where(over > 0, k * (rounds - CAP) + over, 0)
-    info[0] = main
-    info[1] = spare
-    tall = shares[0].shape[0]
+        index += jnp.where(over > 0, k * (rounds - CAP) + over, 0)
+    spare[0] = index
     for place in range(rounds):
         mask = jnp.int32(0)
         for r in range(rounds):
@@ -88,9 +88,16 @@
                     ahead = keys[s] <= keys[r] if s < r else keys[s] < keys[r]
                     rank += ahead.astype(jnp.int32)
             mask += jnp.where(rank == place, masks[r], 0)
-        z_mask = (mask >> 3) & 3
-        info[2 + place] = mask & 1
-        info[2 + rounds + place] = my_z ^ z_mask
+        info[place] = mask & 1
+        info[rounds + place] = (mask >> 3) & 3
+        info[2 * rounds + place] = my_z ^ ((mask >> 3) & 3)
+
+
+def pick_kernel(rounds, info, *refs):
+    shares, stack = refs[:4], refs[4]
+    tall = shares[0].shape[0]
+    for place in range(rounds):
+        z_mask = info[rounds + place]
         for z in range(4):
 
             @pl.when(z_mask == z)
@@ -141,7 +148,7 @@
         near_weights = []
         far_weights = []
         for place in range(rounds):
-            apart = info[2 + place] == 1
+            apart = info[place] == 1
             span_rows = slice(place * share, (place + 1) * share)
             products = jnp.where(apart, far[span_rows], near[span_rows])
             weights = scale * jax.nn.sigmoid(scale * products + bias)
@@ -186,7 +193,7 @@
         out_shape=jax.ShapeDtypeStruct((2 * share, span), jnp.float32),
         in_specs=[smem, smem, vmem, vmem, vmem, vmem],
         out_specs=vmem,
-        compiler_params=pltpu.CompilerParams(vmem_limit_bytes=VMEM_LIMIT),
+        compiler_params=pltpu.CompilerParams(vmem_limit_bytes=OWN_VMEM),
     )(
         trained_steepness,
         learned_shift,
@@ -195,22 +202,30 @@
         picture_vectors,
         sentence_vectors,
     )
-    stack, info = pl.pallas_call(
+    main, spare, info = pl.pallas_call(
+        functools.partial(order_kernel, rounds),
+        out_shape=[
+            jax.ShapeDtypeStruct((1,), jnp.int32),
+            jax.ShapeDtypeStruct((1,), jnp.int32),
+            jax.ShapeDtypeStruct((3 * rounds,), jnp.int32),
+        ],
+        in_specs=[smem],
+        out_specs=[smem, smem, smem],
+    )(partner_table)
+    stack = pl.pallas_call(
         functools.partial(pick_kernel, rounds),
-        out_shape=[
-            jax.ShapeDtypeStruct((rounds * 2 * share, span), jnp.bfloat16),
-            jax.ShapeDtypeStruct((2 + 2 * rounds,), jnp.int32),
-        ],
+        out_shape=jax.ShapeDtypeStruct((rounds * 2 * share, span), jnp.bfloat16),
         in_specs=[smem] + [vmem] * 4,
-        out_specs=[vmem, smem],
-    )(partner_table, *by_z)
-    stack = exchange_x(rounds, info[0], info[1], stack)
+        out_specs=vmem,
+        compiler_params=pltpu.CompilerParams(vmem_limit_bytes=PICK_VMEM),
+    )(info, *by_z)
+    stack = exchange_x(rounds, main[0], spare[0], stack)
     back = pl.pallas_call(
         functools.partial(grad_kernel, rounds),
         out_shape=jax.ShapeDtypeStruct((rounds * 2 * share, span), jnp.float32),
         in_specs=[smem, smem, smem] + [vmem] * 5,
         out_specs=vmem,
-        compiler_params=pltpu.CompilerParams(vmem_limit_bytes=VMEM_LIMIT),
+        compiler_params=pltpu.CompilerParams(vmem_limit_bytes=GRAD_VMEM),
     )(
         info,
         trained_steepness,
@@ -221,10 +236,10 @@
         other_pictures,
         other_texts,
     )
-    back = exchange_x(rounds, info[0], info[1], back.astype(jnp.float16))
+    back = exchange_x(rounds, main[0], spare[0], back.astype(jnp.float16))
 
     back = back.reshape(rounds, 2 * share, span).astype(jnp.float32)
-    homes = info[2 + rounds :]
+    homes = info[2 * rounds :]
     sums = jnp.stack(
         [
             jnp.sum(jnp.where((homes == z)[:, None, None], back, 0.0), axis=0).astype(jnp.float16)
@@ -233,8 +248,10 @@
         axis=0,
     )
     arrived = lax.all_to_all(sums, "wide", 0, 0, axis_index_groups=Z_SETS)
-    slopes = own + jnp.sum(arrived.astype(jnp.float32), axis=0)
-    return slopes[:share], slopes[share:]
+    arrived = arrived.astype(jnp.float32)
+    photo_slopes = own[:share] + jnp.sum(arrived[:, :share], axis=0)
+    wording_slopes = own[share:] + jnp.sum(arrived[:, share:], axis=0)
+    return photo_slopes, wording_slopes
 
 
 def solution(mesh):

time: 152 us -> 138 us (0.908)
  the two profiles are of different devices: /device:TPU:129 before, /device:TPU:8 now
where the time goes in v1:
time: 138 us; the launch traced here: 137 us
  starting transfers between devices  52 us (38%)
  waiting for transfers between devices  50.9 us (37%)
  local copies, waits for them, and re-layouts  10.4 us (8%)
  Pallas kernels  10.4 us (8%)
  other arithmetic  10.1 us (7%)
  between operations  3.37 us (2%)
    ppermute x3, starting transfers between devices, local(): lax.ppermute(shares, 'wide', xor_pairs(8 * mask))  22.9 us
    all_to_all x1, waiting for transfers between devices, local(): arrived = lax.all_to_all(sums, 'wide', 0, 0, axis_index_groups=Z_SETS)  16 us
    ppermute x2, waiting for transfers between devices, move_along_x(): moved[mask] = lax.ppermute(piece, 'wide', xor_pairs(2 * mask))  12.9 us
    ppermute x3, waiting for transfers between devices, local(): lax.ppermute(shares, 'wide', xor_pairs(8 * mask))  12.5 us
    ppermute x2, waiting for transfers between devices, move_spare(): moved = lax.ppermute(stack[:cut], 'wide', xor_pairs(2 * mask))  9.52 us
    ppermute x2, starting transfers between devices, move_spare(): moved = lax.ppermute(stack[:cut], 'wide', xor_pairs(2 * mask))  9.33 us
    ppermute x2, starting transfers between devices, move_along_x(): moved[mask] = lax.ppermute(piece, 'wide', xor_pairs(2 * mask))  9.33 us
    pallas_call x1, Pallas kernels, local(): pl.pallas_call(functools.partial(grad_kernel, rounds), out_shape=jax.Shap...  6.14 us
  transfers between devices with their start and end apart: 10, of which 6 were waited for; matrix products, arithmetic and copies ran while one was open for 5% of the time, Pallas kernels for 3%

profile of v1, /device:TPU:8, one launch (start us, length us, event | category | flops | bytes accessed | tf_op | source)
XLA Modules:
  0.0 137.2 jit_solution(13812152550519646528)
XLA Ops:
  0.6 1.9 %collective-permute-start.123 = (bf16[768,1152]{1,0:T(8,128)(2,1)}, bf16[768,1152]{1,0:T(8,128)(2,1)}, u32[]{:S(2)}, u32[]{:S(2)}) collective-permute-start(bf16[768,1152]{1,0:T(8,128)(2,1)} %pictures.3), channel_id=1, source_target_pairs={{0,24},{24,0},{48,72},{72,48},{96,120},{120,96},{144,168},{168,144... | collective-permute-start | bytes 5308424 | tf_op jit(solution)/shard_map/ppermute | solution.py:181
  2.6 2.4 %collective-permute-start.124 = (bf16[768,1152]{1,0:T(8,128)(2,1)}, bf16[768,1152]{1,0:T(8,128)(2,1)}, u32[]{:S(2)}, u32[]{:S(2)}) collective-permute-start(bf16[768,1152]{1,0:T(8,128)(2,1)} %texts.3), channel_id=1, source_target_pairs={{0,24},{24,0},{48,72},{72,48},{96,120},{120,96},{144,168},{168,144... | collective-permute-start | bytes 5308424 | tf_op jit(solution)/shard_map/ppermute | solution.py:182
  5.0 0.9 constant_dynamic-slice_fusion
  5.9 0.9 constant_dynamic-slice_fusion.1
  6.8 0.0 copy-start.2
  6.8 7.9 %collective-permute-start.120 = (bf16[64,1152]{1,0:T(8,128)(2,1)S(1)}, bf16[64,1152]{1,0:T(8,128)(2,1)S(1)}, u32[]{:S(2)}, u32[]{:S(2)}) collective-permute-start(bf16[64,1152]{1,0:T(8,128)(2,1)S(1)} %pad_maximum_fusion.69.shares.refs_0_), channel_id=1, source_target_pairs={{0,192},{24,216},{48,240},{72,264},{96,288},{120,312},{144,336},{1... | collective-permute-start | bytes 442376 | tf_op jit(solution)/shard_map/ppermute | solution.py:190
  14.7 13.0 %collective-permute-start.121 = (bf16[64,1152]{1,0:T(8,128)(2,1)S(1)}, bf16[64,1152]{1,0:T(8,128)(2,1)S(1)}, u32[]{:S(2)}, u32[]{:S(2)}) collective-permute-start(bf16[64,1152]{1,0:T(8,128)(2,1)S(1)} %pad_maximum_fusion.69.shares.refs_0_), channel_id=1, source_target_pairs={{0,384},{24,408},{48,432},{72,456},{96,480},{120,504},{144,528},{1... | collective-permute-start | bytes 442376 | tf_op jit(solution)/shard_map/ppermute | solution.py:190
  27.8 1.9 %collective-permute-start.122 = (bf16[64,1152]{1,0:T(8,128)(2,1)S(1)}, bf16[64,1152]{1,0:T(8,128)(2,1)S(1)}, u32[]{:S(2)}, u32[]{:S(2)}) collective-permute-start(bf16[64,1152]{1,0:T(8,128)(2,1)S(1)} %pad_maximum_fusion.69.shares.refs_0_), channel_id=1, source_target_pairs={{0,576},{24,600},{48,624},{72,648},{96,672},{120,696},{144,720},{1... | collective-permute-start | bytes 442376 | tf_op jit(solution)/shard_map/ppermute | solution.py:190
  29.7 1.4 %shard_map.78 = (s32[1]{0:T(128)}, s32[1]{0:T(128)}, s32[15]{0:T(128)}) custom-call(s32[5,32]{1,0:T(8,128)} %table.1), custom_call_target="tpu_custom_call" | custom-call | tf_op jit(solution)/shard_map/pallas_call | solution.py:205
  33.6 1.2 broadcast_compare_fusion
  34.8 0.0 collective-permute-done.120.refs_1_
  34.8 0.0 collective-permute-done.121.refs_2_
  34.8 12.5 %collective-permute-done.122.refs_3_ = bf16[64,1152]{1,0:T(8,128)(2,1)S(1)} collective-permute-done((bf16[64,1152]{1,0:T(8,128)(2,1)S(1)}, bf16[64,1152]{1,0:T(8,128)(2,1)S(1)}, u32[]{:S(2)}, u32[]{:S(2)}) %collective-permute-start.122) | collective-permute-done | bytes 147488 | tf_op jit(solution)/shard_map/ppermute | solution.py:190
  47.3 0.0 copy-start.6
  47.3 0.6 copy-done.6
  48.0 0.7 shard_map.79
  48.7 0.0 copy-done.2
  48.7 12.2 %conditional.4 = (bf16[320,1152]{1,0:T(8,128)(2,1)S(1)}) conditional(s32[]{:T(128)} %bitcast.1, bf16[320,1152]{1,0:T(8,128)(2,1)S(1)} %shard_map.79, bf16[320,1152]{1,0:T(8,128)(2,1)S(1)} %shard_map.79, bf16[320,1152]{1,0:T(8,128)(2,1)S(1)} %shard_map.79, bf16[320,1152]{1,0:T(8,128)(2,1)S(1)} %shard_map.79, ...), branch_computations={%region_0.0_spmd, %region_1.0_spmd, %region_2.0_spmd, %region_3.0_... | conditional | flops 2949120 | bytes 5898368 | solution.py:53
  48.8 4.7 %collective-permute-start.1 = (bf16[128,1152]{1,0:T(8,128)(2,1)S(1)}, bf16[128,1152]{1,0:T(8,128)(2,1)S(1)}, u32[]{:S(2)}, u32[]{:S(2)}) collective-permute-start(bf16[128,1152]{1,0:T(8,128)(2,1)S(1)} %slice.377), channel_id=1, source_target_pairs={{0,144},{24,168},{48,96},{72,120},{96,48},{120,72},{144,0},{168,24... | collective-permute-start | bytes 884744 | tf_op jit(solution)/shard_map/cond/branch_2_fun/ppermute | solution.py:41
  53.5 7.3 %collective-permute-done.1 = bf16[128,1152]{1,0:T(8,128)(2,1)S(1)} collective-permute-done((bf16[128,1152]{1,0:T(8,128)(2,1)S(1)}, bf16[128,1152]{1,0:T(8,128)(2,1)S(1)}, u32[]{:S(2)}, u32[]{:S(2)}) %collective-permute-start.1) | collective-permute-done | bytes 294944 | tf_op jit(solution)/shard_map/cond/branch_2_fun/ppermute | solution.py:41
  60.8 0.1 pad_maximum_fusion.1
  60.9 0.0 copy-start.8
  60.9 0.9 copy-done.8
  61.8 13.3 %conditional.5 = (bf16[320,1152]{1,0:T(8,128)(2,1)}) conditional(s32[]{:T(128)} %bitcast, bf16[320,1152]{1,0:T(8,128)(2,1)} %copy-done.8, bf16[320,1152]{1,0:T(8,128)(2,1)} %copy-done.8, bf16[320,1152]{1,0:T(8,128)(2,1)} %copy-done.8, bf16[320,1152]{1,0:T(8,128)(2,1)} %copy-done.8, ...), branch_computations={%region_26.0_spmd, %region_27.0_spmd, %region_28.0_spmd, %region_2... | conditional | flops 1474560 | bytes 4718640 | solution.py:58
  61.8 1.1 slice.461
  62.9 4.7 %collective-permute-start.13 = (bf16[128,1152]{1,0:T(8,128)(2,1)S(1)}, bf16[128,1152]{1,0:T(8,128)(2,1)S(1)}, u32[]{:S(2)}, u32[]{:S(2)}) collective-permute-start(bf16[128,1152]{1,0:T(8,128)(2,1)S(1)} %slice.461), channel_id=1, source_target_pairs={{0,144},{24,168},{48,96},{72,120},{96,48},{120,72},{144,0},{168,24... | collective-permute-start | bytes 884744 | tf_op jit(solution)/shard_map/cond/branch_8_fun/ppermute | solution.py:48
  67.6 1.0 slice.462
  68.6 5.5 %collective-permute-done.13 = bf16[128,1152]{1,0:T(8,128)(2,1)S(1)} collective-permute-done((bf16[128,1152]{1,0:T(8,128)(2,1)S(1)}, bf16[128,1152]{1,0:T(8,128)(2,1)S(1)}, u32[]{:S(2)}, u32[]{:S(2)}) %collective-permute-start.13) | collective-permute-done | bytes 294944 | tf_op jit(solution)/shard_map/cond/branch_8_fun/ppermute | solution.py:48
  74.1 0.9 pad_maximum_fusion.32
  75.0 0.0 collective-permute-done.123.other_pictures
  75.0 0.0 collective-permute-done.124.other_texts
  75.0 0.0 copy-done
  75.0 0.0 copy-done.1
  75.1 0.0 copy-done.7
  75.1 6.1 %shard_map.80 = f32[320,1152]{1,0:T(8,128)S(1)} custom-call(s32[15]{0:T(128)S(1)} %copy-done.7, f32[1]{0:T(128)S(6)} %copy.80.steepness, f32[1]{0:T(128)S(6)} %copy.81.shift, bf16[320,1152]{1,0:T(8,128)(2,1)} %get-tuple-element.263.stack, bf16[768,1152]{1,0:T(8,128)(2,1)S(1)} %copy-done.1, bf16[768,1152]{1,0:T(8,128)(2,1)S(1)} %copy-done, ...), custom_call_target="tpu_custom_call" | custom-call | tf_op jit(solution)/shard_map/pallas_call | solution.py:223
  81.2 0.9 convert_element_type.164
  82.1 12.4 %conditional.6 = (f16[320,1152]{1,0:T(8,128)(2,1)}) conditional(s32[]{:T(128)} %bitcast.1, f16[320,1152]{1,0:T(8,128)(2,1)} %convert_element_type.164, f16[320,1152]{1,0:T(8,128)(2,1)} %convert_element_type.164, f16[320,1152]{1,0:T(8,128)(2,1)} %convert_element_type.164, ...), branch_computations={%region_36.0_spmd, %region_37.0_spmd, %region_38.0_spmd, %region_3... | conditional | flops 1105920 | bytes 5898368 | solution.py:53
  82.1 1.1 slice.468
  83.2 4.7 %collective-permute-start.16 = (f16[128,1152]{1,0:T(8,128)(2,1)S(1)}, f16[128,1152]{1,0:T(8,128)(2,1)S(1)}, u32[]{:S(2)}, u32[]{:S(2)}) collective-permute-start(f16[128,1152]{1,0:T(8,128)(2,1)S(1)} %slice.468), channel_id=1, source_target_pairs={{0,144},{24,168},{48,96},{72,120},{96,48},{120,72},{144,0},{168,24... | collective-permute-start | bytes 884744 | tf_op jit(solution)/shard_map/cond/branch_2_fun/ppermute | solution.py:41
  87.9 5.6 %collective-permute-done.16 = f16[128,1152]{1,0:T(8,128)(2,1)S(1)} collective-permute-done((f16[128,1152]{1,0:T(8,128)(2,1)S(1)}, f16[128,1152]{1,0:T(8,128)(2,1)S(1)}, u32[]{:S(2)}, u32[]{:S(2)}) %collective-permute-start.16) | collective-permute-done | bytes 294944 | tf_op jit(solution)/shard_map/cond/branch_2_fun/ppermute | solution.py:41
  93.5 0.0 slice-done.1
  93.5 1.0 pad_maximum_fusion.35
  94.5 11.9 %conditional.7 = (f16[320,1152]{1,0:T(8,128)(2,1)}) conditional(s32[]{:T(128)} %bitcast, f16[320,1152]{1,0:T(8,128)(2,1)} %get-tuple-element.264, f16[320,1152]{1,0:T(8,128)(2,1)} %get-tuple-element.264, f16[320,1152]{1,0:T(8,128)(2,1)} %get-tuple-element.264, f16[320,1152]{1,0:T(8,128)(2,1)} %get-tuple-element.264, ...), branch_computations={%region_62.0_spmd, %region_63.0_spmd, %region_64.0_spmd, %region_6... | conditional | flops 368640 | bytes 4718640 | solution.py:58
  94.5 1.0 slice.552
  95.5 4.7 %collective-permute-start.28 = (f16[128,1152]{1,0:T(8,128)(2,1)S(1)}, f16[128,1152]{1,0:T(8,128)(2,1)S(1)}, u32[]{:S(2)}, u32[]{:S(2)}) collective-permute-start(f16[128,1152]{1,0:T(8,128)(2,1)S(1)} %slice.552), channel_id=1, source_target_pairs={{0,144},{24,168},{48,96},{72,120},{96,48},{120,72},{144,0},{168,24... | collective-permute-start | bytes 884744 | tf_op jit(solution)/shard_map/cond/branch_8_fun/ppermute | solution.py:48
  100.2 1.1 slice.553
  101.3 4.1 %collective-permute-done.28 = f16[128,1152]{1,0:T(8,128)(2,1)S(1)} collective-permute-done((f16[128,1152]{1,0:T(8,128)(2,1)S(1)}, f16[128,1152]{1,0:T(8,128)(2,1)S(1)}, u32[]{:S(2)}, u32[]{:S(2)}) %collective-permute-start.28) | collective-permute-done | bytes 294944 | tf_op jit(solution)/shard_map/cond/branch_8_fun/ppermute | solution.py:48
  105.4 1.0 pad_maximum_fusion.66
  106.4 0.0 copy-done.10
  106.4 1.8 %fusion = (f32[64,1152]{1,0:T(8,128)S(1)}, f32[64,1152]{1,0:T(8,128)S(1)}, f32[64,1152]{1,0:T(8,128)S(1)}, f32[64,1152]{1,0:T(8,128)S(1)}) fusion(f16[5,64,1152]{2,1,0:T(8,128)(2,1)} %bitcast.12, pred[5]{0:T(512)(128)(4,1)S(1)} %copy-done.10, pred[5]{0:T(512)(128)(4,1)S(1)} %get-tuple-element.255, pred[5]{0:T(512)(128)(4,1)S(1)} %get-tuple-element.256, ...), kind=kLoop, calls=%fused_computation.72 | loop fusion | flops 3022848 | bytes 1916948 | tf_op jit(solution)/shard_map/reduce_sum | solution.py:245
  108.2 0.0 copy-start.9
  108.3 1.0 pad_maximum_fusion.68
  109.3 6.1 %all-to-all-start = ((f16[4,64,1152]{2,1,0:T(8,128)(2,1)}), f16[4,64,1152]{2,1,0:T(8,128)(2,1)}, u32[]{:S(2)}, u32[]{:S(2)}) async-start(f16[4,64,1152]{2,1,0:T(8,128)(2,1)} %pad_maximum_fusion.68), calls=%async_computation | async-start | bytes 1179648 | tf_op jit(solution)/shard_map/all_to_all | solution.py:250
  115.4 0.0 copy-done.9
  115.4 0.0 copy-start.3
  115.4 0.9 copy-done.3
  116.3 2.2 %shard_map.77 = f32[64,1152]{1,0:T(8,128)S(1)} custom-call(f32[1]{0:T(128)S(6)} %copy.80.steepness, f32[1]{0:T(128)S(6)} %copy.81.shift, s32[1,768]{1,0:T(1,128)S(1)} %broadcast_in_dim.37.matched, bf16[64,1152]{1,0:T(8,128)(2,1)S(1)} %copy-done.3, bf16[768,1152]{1,0:T(8,128)(2,1)S(1)} %copy-done.1, bf16[768,1152]{1,0:T(8,128)(2,1)S(1)} %copy-done), custom_call_target="tpu_custom_call" | custom-call | tf_op jit(solution)/shard_map/pallas_call | solution.py:191
  118.5 0.0 copy-start.4
  118.5 0.7 copy-done.4
  119.3 16.0 %all-to-all-done = f16[4,64,1152]{2,1,0:T(8,128)(2,1)} async-done(((f16[4,64,1152]{2,1,0:T(8,128)(2,1)}), f16[4,64,1152]{2,1,0:T(8,128)(2,1)}, u32[]{:S(2)}, u32[]{:S(2)}) %all-to-all-start) | async-done | bytes 589856 | tf_op jit(solution)/shard_map/all_to_all | solution.py:250
  135.2 1.2 convert_element_type.175
  136.4 0.1 slice_reduce_fusion
  136.5 0.0 copy-done.5
  136.5 0.7 slice_add_fusion
  (12 shorter events, 0.2 us)
Async XLA Ops:
  0.6 74.4 %collective-permute-start.123 = (bf16[768,1152]{1,0:T(8,128)(2,1)}, bf16[768,1152]{1,0:T(8,128)(2,1)}, u32[]{:S(2)}, u32[]{:S(2)}) collective-permute-start(bf16[768,1152]{1,0:T(8,128)(2,1)} %pictures.3), channel_id=1, source_target_pairs={{0,24},{24,0},{48,72},{72,48},{96,120},{120,96},{144,168},{168,144... | collective-permute-start | bytes 5308424 | tf_op jit(solution)/shard_map/ppermute | solution.py:181
  2.6 72.5 %collective-permute-start.124 = (bf16[768,1152]{1,0:T(8,128)(2,1)}, bf16[768,1152]{1,0:T(8,128)(2,1)}, u32[]{:S(2)}, u32[]{:S(2)}) collective-permute-start(bf16[768,1152]{1,0:T(8,128)(2,1)} %texts.3), channel_id=1, source_target_pairs={{0,24},{24,0},{48,72},{72,48},{96,120},{120,96},{144,168},{168,144... | collective-permute-start | bytes 5308424 | tf_op jit(solution)/shard_map/ppermute | solution.py:182
  6.8 41.9 %copy-start.2 = (bf16[64,1152]{1,0:T(8,128)(2,1)}, bf16[64,1152]{1,0:T(8,128)(2,1)S(1)}, u32[]{:S(2)}) copy-start(bf16[64,1152]{1,0:T(8,128)(2,1)S(1)} %pad_maximum_fusion.69.shares.refs_0_) | copy-start | bytes 442372
  6.8 28.0 %collective-permute-start.120 = (bf16[64,1152]{1,0:T(8,128)(2,1)S(1)}, bf16[64,1152]{1,0:T(8,128)(2,1)S(1)}, u32[]{:S(2)}, u32[]{:S(2)}) collective-permute-start(bf16[64,1152]{1,0:T(8,128)(2,1)S(1)} %pad_maximum_fusion.69.shares.refs_0_), channel_id=1, source_target_pairs={{0,192},{24,216},{48,240},{72,264},{96,288},{120,312},{144,336},{1... | collective-permute-start | bytes 442376 | tf_op jit(solution)/shard_map/ppermute | solution.py:190
  14.7 20.1 %collective-permute-start.121 = (bf16[64,1152]{1,0:T(8,128)(2,1)S(1)}, bf16[64,1152]{1,0:T(8,128)(2,1)S(1)}, u32[]{:S(2)}, u32[]{:S(2)}) collective-permute-start(bf16[64,1152]{1,0:T(8,128)(2,1)S(1)} %pad_maximum_fusion.69.shares.refs_0_), channel_id=1, source_target_pairs={{0,384},{24,408},{48,432},{72,456},{96,480},{120,504},{144,528},{1... | collective-permute-start | bytes 442376 | tf_op jit(solution)/shard_map/ppermute | solution.py:190
  27.8 19.6 %collective-permute-start.122 = (bf16[64,1152]{1,0:T(8,128)(2,1)S(1)}, bf16[64,1152]{1,0:T(8,128)(2,1)S(1)}, u32[]{:S(2)}, u32[]{:S(2)}) collective-permute-start(bf16[64,1152]{1,0:T(8,128)(2,1)S(1)} %pad_maximum_fusion.69.shares.refs_0_), channel_id=1, source_target_pairs={{0,576},{24,600},{48,624},{72,648},{96,672},{120,696},{144,720},{1... | collective-permute-start | bytes 442376 | tf_op jit(solution)/shard_map/ppermute | solution.py:190
  47.3 0.6 copy-start.6
  48.8 12.0 %collective-permute-start.1 = (bf16[128,1152]{1,0:T(8,128)(2,1)S(1)}, bf16[128,1152]{1,0:T(8,128)(2,1)S(1)}, u32[]{:S(2)}, u32[]{:S(2)}) collective-permute-start(bf16[128,1152]{1,0:T(8,128)(2,1)S(1)} %slice.377), channel_id=1, source_target_pairs={{0,144},{24,168},{48,96},{72,120},{96,48},{120,72},{144,0},{168,24... | collective-permute-start | bytes 884744 | tf_op jit(solution)/shard_map/cond/branch_2_fun/ppermute | solution.py:41
  60.9 0.9 copy-start.8
  61.8 13.3 %copy-start = (bf16[768,1152]{1,0:T(8,128)(2,1)S(1)}, bf16[768,1152]{1,0:T(8,128)(2,1)}, u32[]{:S(2)}) copy-start(bf16[768,1152]{1,0:T(8,128)(2,1)} %texts.3) | copy-start | bytes 5308420
  61.8 13.3 %copy-start.1 = (bf16[768,1152]{1,0:T(8,128)(2,1)S(1)}, bf16[768,1152]{1,0:T(8,128)(2,1)}, u32[]{:S(2)}) copy-start(bf16[768,1152]{1,0:T(8,128)(2,1)} %pictures.3) | copy-start | bytes 5308420
  61.8 13.3 %copy-start.7 = (s32[15]{0:T(128)S(1)}, s32[15]{0:T(128)}, u32[]{:S(2)}) copy-start(s32[15]{0:T(128)} %get-tuple-element.159.info) | copy-start | bytes 184
  62.9 11.2 %collective-permute-start.13 = (bf16[128,1152]{1,0:T(8,128)(2,1)S(1)}, bf16[128,1152]{1,0:T(8,128)(2,1)S(1)}, u32[]{:S(2)}, u32[]{:S(2)}) collective-permute-start(bf16[128,1152]{1,0:T(8,128)(2,1)S(1)} %slice.461), channel_id=1, source_target_pairs={{0,144},{24,168},{48,96},{72,120},{96,48},{120,72},{144,0},{168,24... | collective-permute-start | bytes 884744 | tf_op jit(solution)/shard_map/cond/branch_8_fun/ppermute | solution.py:48
  82.1 11.3 %slice-start.1 = ((f16[320,1152]{1,0:T(8,128)(2,1)}), f16[192,1152]{1,0:T(8,128)(2,1)S(1)}, s32[]{:S(2)}) async-start(f16[320,1152]{1,0:T(8,128)(2,1)} %param.38), calls=%async_computation.2 | async-start | bytes 884736 | tf_op jit(solution)/shard_map/cond/branch_2_fun/slice | solution.py:31
  83.2 10.3 %collective-permute-start.16 = (f16[128,1152]{1,0:T(8,128)(2,1)S(1)}, f16[128,1152]{1,0:T(8,128)(2,1)S(1)}, u32[]{:S(2)}, u32[]{:S(2)}) collective-permute-start(f16[128,1152]{1,0:T(8,128)(2,1)S(1)} %slice.468), channel_id=1, source_target_pairs={{0,144},{24,168},{48,96},{72,120},{96,48},{120,72},{144,0},{168,24... | collective-permute-start | bytes 884744 | tf_op jit(solution)/shard_map/cond/branch_2_fun/ppermute | solution.py:41
  94.5 11.9 %copy-start.10 = (pred[5]{0:T(512)(128)(4,1)S(1)}, pred[5]{0:T(512)(128)(4,1)}, u32[]{:S(2)}) copy-start(pred[5]{0:T(512)(128)(4,1)} %get-tuple-element.257) | copy-start | bytes 19
  95.5 9.8 %collective-permute-start.28 = (f16[128,1152]{1,0:T(8,128)(2,1)S(1)}, f16[128,1152]{1,0:T(8,128)(2,1)S(1)}, u32[]{:S(2)}, u32[]{:S(2)}) collective-permute-start(f16[128,1152]{1,0:T(8,128)(2,1)S(1)} %slice.552), channel_id=1, source_target_pairs={{0,144},{24,168},{48,96},{72,120},{96,48},{120,72},{144,0},{168,24... | collective-permute-start | bytes 884744 | tf_op jit(solution)/shard_map/cond/branch_8_fun/ppermute | solution.py:48
  108.2 7.2 %copy-start.9 = (s32[768]{0:T(1024)S(1)}, s32[768]{0:T(1024)}, u32[]{:S(2)}) copy-start(s32[768]{0:T(1024)} %param.80) | copy-start | bytes 9220
  109.3 25.9 %all-to-all-start = ((f16[4,64,1152]{2,1,0:T(8,128)(2,1)}), f16[4,64,1152]{2,1,0:T(8,128)(2,1)}, u32[]{:S(2)}, u32[]{:S(2)}) async-start(f16[4,64,1152]{2,1,0:T(8,128)(2,1)} %pad_maximum_fusion.68), calls=%async_computation | async-start | bytes 1179648 | tf_op jit(solution)/shard_map/all_to_all | solution.py:250
  115.4 0.9 copy-start.3
  118.5 0.7 copy-start.4
  135.2 1.3 copy-start.5

commit v2 on v1

v2 whole, which is shorter than its diff:
```python
import functools
import jax
import jax.numpy as jnp
from jax import lax
from jax.experimental import pallas as pl
from jax.experimental.pallas import tpu as pltpu
from jax.sharding import PartitionSpec as P

WIDE = 32
Z_SETS = [[low + 8 * z for z in range(4)] for low in range(8)]
X_SETS = [[8 * z + 2 * x + core for x in range(4)] for z in range(4) for core in range(2)]
CAP = 2
MAIN = 4 * CAP
PICK_VMEM = 8 * 1024 * 1024
OWN_VMEM = 12 * 1024 * 1024
GRAD_VMEM = 24 * 1024 * 1024


def xor_pairs(mask):
    return [(i, i ^ mask) for i in range(WIDE)]


def move_spare(mask, count, stack):
    moved = lax.ppermute(stack[:count], "wide", xor_pairs(2 * mask))
    return jnp.concatenate([moved, stack[count:]], axis=0) if count < stack.shape[0] else moved


def exchange_x(spare, main, rest):
    places, tall, span = main.shape
    sent = main.reshape(4, CAP * tall, span)
    main = lax.all_to_all(sent, "wide", 0, 0, axis_index_groups=X_SETS).reshape(places, tall, span)
    moves = [lambda stack: stack]
    for mask in (1, 2, 3):
        for count in range(1, rest.shape[0] + 1):
            moves.append(functools.partial(move_spare, mask, count))
    return main, lax.switch(spare, moves, rest)


def order_kernel(rounds, table, spare, info, homes):
    my_z = lax.axis_index("wide") // 8
    my_x = (lax.axis_index("wide") // 2) % 4
    masks = [table[r, 0] & (WIDE - 1) for r in range(rounds)]
    x_masks = [(mask >> 1) & 3 for mask in masks]
    for place in range(MAIN + rounds - CAP):
        homes[place] = -1
    beyond = jnp.int32(0)
    index = jnp.int32(0)
    for r in range(rounds):
        before = sum([(x_masks[s] == x_masks[r]).astype(jnp.int32) for s in range(r)], jnp.int32(0))
        fits = before < CAP
        place = jnp.where(fits, (my_x ^ x_masks[r]) * CAP + before, MAIN + beyond)
        beyond += jnp.where(fits, 0, 1)
        over = before - CAP + 1
        index = jnp.where(fits | (x_masks[r] == 0), index, (x_masks[r] - 1) * (rounds - CAP) + over)
        info[r] = masks[r] & 1
        info[rounds + r] = masks[r] >> 3
        info[2 * rounds + r] = place
        homes[place] = my_z ^ (masks[r] >> 3)
    spare[0] = index


def pick_kernel(rounds, info, *refs):
    shares, (main, rest) = refs[:4], refs[4:]
    main[...] = jnp.zeros_like(main)
    rest[...] = jnp.zeros_like(rest)
    for r in range(rounds):
        z_mask = info[rounds + r]
        place = info[2 * rounds + r]
        for z in range(4):

            @pl.when((z_mask == z) & (place < MAIN))
            def _():
                main[place] = shares[z][...]

            @pl.when((z_mask == z) & (place >= MAIN))
            def _():
                rest[place - MAIN] = shares[z][...]


def dot_last(left, right):
    return lax.dot_general(left, right, (((1,), (1,)), ((), ())), preferred_element_type=jnp.float32)


def dot(left, right):
    return jnp.dot(left, right, preferred_element_type=jnp.float32)


def own_kernel(steepness, shift, matched, shares, pictures, texts, own):
    rows, span = pictures.shape
    share = own.shape[0] // 2
    first = lax.axis_index("wide") * rows
    begin = lax.axis_index("narrow") * share
    scale = steepness[0] / span
    bias = shift[0]
    lanes = lax.broadcasted_iota(jnp.int32, (share, rows), 1)
    mine = begin + lax.broadcasted_iota(jnp.int32, (share, rows), 0)
    matches = jnp.broadcast_to(matched[...], (share, rows))
    my_match = jnp.sum(jnp.where(lanes == mine, matches, 0), axis=1, keepdims=True)
    for kind, block in enumerate([texts, pictures]):
        span_rows = slice(kind * share, (kind + 1) * share)
        same = (my_match == first + lanes) if kind == 0 else (matches == first + mine)
        signs = jnp.where(same, 1.0, -1.0).astype(jnp.float32)
        logits = scale * dot_last(shares[span_rows, :], block[...]) + bias
        weights = (-scale * signs * jax.nn.sigmoid(-signs * logits)).astype(jnp.bfloat16)
        own[span_rows, :] = dot(weights, block[...])


def grad_kernel(
    rounds,
    info,
    steepness,
    shift,
    main,
    rest,
    pictures,
    texts,
    other_pictures,
    other_texts,
    back_main,
    back_rest,
    left,
):
    span = pictures.shape[1]
    share = main.shape[1] // 2
    scale = steepness[0] / span
    bias = shift[0]
    back_main[...] = jnp.zeros_like(back_main)
    back_rest[...] = jnp.zeros_like(back_rest)
    for r in range(rounds):
        place = info[2 * rounds + r]
        for kind in range(2):
            kind_rows = slice(kind * share, (kind + 1) * share)
            left_rows = slice(r * share, (r + 1) * share)

            @pl.when(place < MAIN)
            def _():
                left[kind, left_rows, :] = main[place, kind_rows, :]

            @pl.when(place >= MAIN)
            def _():
                left[kind, left_rows, :] = rest[place - MAIN, kind_rows, :]

    for kind, (block, other) in enumerate([(texts, other_texts), (pictures, other_pictures)]):
        kind_rows = slice(kind * share, (kind + 1) * share)
        near = dot_last(left[kind], block[...])
        far = dot_last(left[kind], other[...])
        near_weights = []
        far_weights = []
        for r in range(rounds):
            apart = info[r] == 1
            left_rows = slice(r * share, (r + 1) * share)
            products = jnp.where(apart, far[left_rows], near[left_rows])
            weights = scale * jax.nn.sigmoid(scale * products + bias)
            near_weights.append(jnp.where(apart, 0.0, weights).astype(jnp.bfloat16))
            far_weights.append(jnp.where(apart, weights, 0.0).astype(jnp.bfloat16))
        slopes = dot(jnp.concatenate(near_weights, axis=0), block[...]) + dot(
            jnp.concatenate(far_weights, axis=0), other[...]
        )
        for r in range(rounds):
            place = info[2 * rounds + r]
            slope = slopes[r * share : (r + 1) * share]

            @pl.when(place < MAIN)
            def _():
                back_main[place, kind_rows, :] = slope

            @pl.when(place >= MAIN)
            def _():
                back_rest[place - MAIN, kind_rows, :] = slope


def local(
    picture_vectors,
    sentence_vectors,
    matched_text_indices,
    partner_table,
    trained_steepness,
    learned_shift,
):
    rows, span = picture_vectors.shape
    rounds = partner_table.shape[0]
    share = rows // lax.axis_size("narrow")
    begin = lax.axis_index("narrow") * share
    smem = pl.BlockSpec(memory_space=pltpu.SMEM)
    vmem = pl.BlockSpec(memory_space=pltpu.VMEM)

    other_pictures = lax.ppermute(picture_vectors, "wide", xor_pairs(1))
    other_texts = lax.ppermute(sentence_vectors, "wide", xor_pairs(1))
    shares = jnp.concatenate(
        [
            lax.dynamic_slice_in_dim(picture_vectors, begin, share, 0),
            lax.dynamic_slice_in_dim(sentence_vectors, begin, share, 0),
        ],
        axis=0,
    )
    by_z = [shares] + [lax.ppermute(shares, "wide", xor_pairs(8 * mask)) for mask in (1, 2, 3)]
    own = pl.pallas_call(
        own_kernel,
        out_shape=jax.ShapeDtypeStruct((2 * share, span), jnp.float32),
        in_specs=[smem, smem, vmem, vmem, vmem, vmem],
        out_specs=vmem,
        compiler_params=pltpu.CompilerParams(vmem_limit_bytes=OWN_VMEM),
    )(
        trained_steepness,
        learned_shift,
        matched_text_indices[None, :],
        shares,
        picture_vectors,
        sentence_vectors,
    )
    spare, info, homes = pl.pallas_call(
        functools.partial(order_kernel, rounds),
        out_shape=[
            jax.ShapeDtypeStruct((1,), jnp.int32),
            jax.ShapeDtypeStruct((3 * rounds,), jnp.int32),
            jax.ShapeDtypeStruct((MAIN + rounds - CAP,), jnp.int32),
        ],
        in_specs=[smem],
        out_specs=[smem, smem, smem],
        compiler_params=pltpu.CompilerParams(vmem_limit_bytes=PICK_VMEM),
    )(partner_table)
    main_shape = (MAIN, 2 * share, span)
    rest_shape = (rounds - CAP, 2 * share, span)
    main, rest = pl.pallas_call(
        functools.partial(pick_kernel, rounds),
        out_shape=[
            jax.ShapeDtypeStruct(main_shape, jnp.bfloat16),
            jax.ShapeDtypeStruct(rest_shape, jnp.bfloat16),
        ],
        in_specs=[smem] + [vmem] * 4,
        out_specs=[vmem, vmem],
        compiler_params=pltpu.CompilerParams(vmem_limit_bytes=PICK_VMEM),
    )(info, *by_z)
    main, rest = exchange_x(spare[0], main, rest)
    main, rest = pl.pallas_call(
        functools.partial(grad_kernel, rounds),
        out_shape=[
            jax.ShapeDtypeStruct(main_shape, jnp.float32),
            jax.ShapeDtypeStruct(rest_shape, jnp.float32),
        ],
        in_specs=[smem, smem, smem] + [vmem] * 6,
        out_specs=[vmem, vmem],
        scratch_shapes=[pltpu.VMEM((2, rounds * share, span), jnp.bfloat16)],
        compiler_params=pltpu.CompilerParams(vmem_limit_bytes=GRAD_VMEM),
    )(
        info,
        trained_steepness,
        learned_shift,
        main,
        rest,
        picture_vectors,
        sentence_vectors,
        other_pictures,
        other_texts,
    )
    main, rest = exchange_x(spare[0], main.astype(jnp.float16), rest.astype(jnp.float16))

    def of_home(z):
        mine = (homes == z)[:, None, None]
        return (
            jnp.sum(jnp.where(mine[:MAIN], main.astype(jnp.float32), 0.0), axis=0)
            + jnp.sum(jnp.where(mine[MAIN:], rest.astype(jnp.float32), 0.0), axis=0)
        ).astype(jnp.float16)

    sums = jnp.stack([of_home(z) for z in range(4)], axis=0)
    arrived = lax.all_to_all(sums, "wide", 0, 0, axis_index_groups=Z_SETS)
    arrived = arrived.astype(jnp.float32)
    photo_slopes = own[:share] + jnp.sum(arrived[:, :share], axis=0)
    wording_slopes = own[share:] + jnp.sum(arrived[:, share:], axis=0)
    return photo_slopes, wording_slopes


def solution(mesh):
    in_specs = (P("wide", None), P("wide", None), P("wide"), P(), P(), P())
    out_specs = (P(("wide", "narrow"), None), P(("wide", "narrow"), None))
    return jax.shard_map(local, mesh=mesh, in_specs=in_specs, out_specs=out_specs, check_vma=False)
```

time: 138 us -> 146 us (1.058)
  the two profiles are of different devices: /device:TPU:8 before, /device:TPU:64 now
where the time goes in v2:
time: 146 us; the launch traced here: 145 us
  starting transfers between devices  55.5 us (38%)
  waiting for transfers between devices  48.5 us (33%)
  other arithmetic  13.2 us (9%)
  Pallas kernels  12.7 us (9%)
  local copies, waits for them, and re-layouts  11.8 us (8%)
  between operations  2.87 us (2%)
    all_to_all x1, waiting for transfers between devices, local(): arrived = lax.all_to_all(sums, 'wide', 0, 0, axis_index_groups=Z_SETS)  21.9 us
    ppermute x3, starting transfers between devices, local(): lax.ppermute(shares, 'wide', xor_pairs(8 * mask))  21.4 us
    ppermute x2, waiting for transfers between devices, move_spare(): moved = lax.ppermute(stack[:count], 'wide', xor_pairs(2 * mask))  15.1 us
    ppermute x3, waiting for transfers between devices, local(): lax.ppermute(shares, 'wide', xor_pairs(8 * mask))  11.6 us
    ppermute x2, starting transfers between devices, move_spare(): moved = lax.ppermute(stack[:count], 'wide', xor_pairs(2 * mask))  10.8 us
    all_to_all x1, starting transfers between devices, local(): arrived = lax.all_to_all(sums, 'wide', 0, 0, axis_index_groups=Z_SETS)  10.4 us
    all_to_all x2, starting transfers between devices, exchange_x(): lax.all_to_all(sent, 'wide', 0, 0, axis_index_groups=X_SETS)  8.56 us
    pallas_call x1, Pallas kernels, local(): pl.pallas_call(functools.partial(grad_kernel, rounds), out_shape=[jax.Sha...  7.09 us
  transfers between devices with their start and end apart: 10, of which 5 were waited for; matrix products, arithmetic and copies ran while one was open for 10% of the time, Pallas kernels for 4%

profile of v2, /device:TPU:64, one launch (start us, length us, event | category | flops | bytes accessed | tf_op | source)
XLA Modules:
  0.0 144.7 jit_solution(4513722400224054756)
XLA Ops:
  0.6 1.9 %collective-permute-start.21 = (bf16[768,1152]{1,0:T(8,128)(2,1)}, bf16[768,1152]{1,0:T(8,128)(2,1)}, u32[]{:S(2)}, u32[]{:S(2)}) collective-permute-start(bf16[768,1152]{1,0:T(8,128)(2,1)} %pictures.3), channel_id=1, source_target_pairs={{0,24},{24,0},{48,72},{72,48},{96,120},{120,96},{144,168},{168,144... | collective-permute-start | bytes 5308424 | tf_op jit(solution)/shard_map/ppermute | solution.py:187
  2.6 2.4 %collective-permute-start.22 = (bf16[768,1152]{1,0:T(8,128)(2,1)}, bf16[768,1152]{1,0:T(8,128)(2,1)}, u32[]{:S(2)}, u32[]{:S(2)}) collective-permute-start(bf16[768,1152]{1,0:T(8,128)(2,1)} %texts.3), channel_id=1, source_target_pairs={{0,24},{24,0},{48,72},{72,48},{96,120},{120,96},{144,168},{168,144... | collective-permute-start | bytes 5308424 | tf_op jit(solution)/shard_map/ppermute | solution.py:188
  5.0 0.9 constant_dynamic-slice_fusion
  5.9 0.9 constant_dynamic-slice_fusion.1
  6.8 9.1 %collective-permute-start.18 = (bf16[64,1152]{1,0:T(8,128)(2,1)S(1)}, bf16[64,1152]{1,0:T(8,128)(2,1)S(1)}, u32[]{:S(2)}, u32[]{:S(2)}) collective-permute-start(bf16[64,1152]{1,0:T(8,128)(2,1)S(1)} %pad_maximum_fusion.13.shares.refs_0_), channel_id=1, source_target_pairs={{0,192},{24,216},{48,240},{72,264},{96,288},{120,312},{144,336},{1... | collective-permute-start | bytes 442376 | tf_op jit(solution)/shard_map/ppermute | solution.py:196
  15.9 10.3 %collective-permute-start.19 = (bf16[64,1152]{1,0:T(8,128)(2,1)S(1)}, bf16[64,1152]{1,0:T(8,128)(2,1)S(1)}, u32[]{:S(2)}, u32[]{:S(2)}) collective-permute-start(bf16[64,1152]{1,0:T(8,128)(2,1)S(1)} %pad_maximum_fusion.13.shares.refs_0_), channel_id=1, source_target_pairs={{0,384},{24,408},{48,432},{72,456},{96,480},{120,504},{144,528},{1... | collective-permute-start | bytes 442376 | tf_op jit(solution)/shard_map/ppermute | solution.py:196
  26.2 1.9 %collective-permute-start.20 = (bf16[64,1152]{1,0:T(8,128)(2,1)S(1)}, bf16[64,1152]{1,0:T(8,128)(2,1)S(1)}, u32[]{:S(2)}, u32[]{:S(2)}) collective-permute-start(bf16[64,1152]{1,0:T(8,128)(2,1)S(1)} %pad_maximum_fusion.13.shares.refs_0_), channel_id=1, source_target_pairs={{0,576},{24,600},{48,624},{72,648},{96,672},{120,696},{144,720},{1... | collective-permute-start | bytes 442376 | tf_op jit(solution)/shard_map/ppermute | solution.py:196
  28.2 0.0 copy-start.7
  28.2 0.7 copy-done.7
  28.9 1.3 shard_map.78
  30.1 0.0 collective-permute-done.18.refs_1_
  30.2 9.7 %collective-permute-done.19.refs_2_ = bf16[64,1152]{1,0:T(8,128)(2,1)S(1)} collective-permute-done((bf16[64,1152]{1,0:T(8,128)(2,1)S(1)}, bf16[64,1152]{1,0:T(8,128)(2,1)S(1)}, u32[]{:S(2)}, u32[]{:S(2)}) %collective-permute-start.19) | collective-permute-done | bytes 147488 | tf_op jit(solution)/shard_map/ppermute | solution.py:196
  39.8 1.9 %collective-permute-done.20.refs_3_ = bf16[64,1152]{1,0:T(8,128)(2,1)S(1)} collective-permute-done((bf16[64,1152]{1,0:T(8,128)(2,1)S(1)}, bf16[64,1152]{1,0:T(8,128)(2,1)S(1)}, u32[]{:S(2)}, u32[]{:S(2)}) %collective-permute-start.20) | collective-permute-done | bytes 147488 | tf_op jit(solution)/shard_map/ppermute | solution.py:196
  41.7 2.2 %shard_map.79 = (bf16[8,64,1152]{2,1,0:T(8,128)(2,1)}, bf16[3,64,1152]{2,1,0:T(8,128)(2,1)}) custom-call(s32[15]{0:T(128)S(1)} %get-tuple-element.58.info, bf16[64,1152]{1,0:T(8,128)(2,1)S(1)} %pad_maximum_fusion.13.shares.refs_0_, bf16[64,1152]{1,0:T(8,128)(2,1)S(1)} %collective-permute-done.18.refs_1_, ...), custom_call_target="tpu_custom_call" | custom-call | tf_op jit(solution)/shard_map/pallas_call | solution.py:224
  43.9 0.7 copy-done.2
  44.6 4.3 %all-to-all-start = ((bf16[4,128,1152]{2,1,0:T(8,128)(2,1)}), bf16[4,128,1152]{2,1,0:T(8,128)(2,1)}, u32[]{:S(2)}, u32[]{:S(2)}) async-start(bf16[4,128,1152]{2,1,0:T(8,128)(2,1)} %bitcast), calls=%async_computation | async-start | bytes 2359296 | tf_op jit(solution)/shard_map/all_to_all | solution.py:31
  50.8 0.0 copy-start
  50.8 0.0 copy-start.1
  50.8 17.7 %conditional.2 = (bf16[3,64,1152]{2,1,0:T(8,128)(2,1)}) conditional(s32[]{:T(128)} %bitcast.2, bf16[3,64,1152]{2,1,0:T(8,128)(2,1)} %get-tuple-element.61, bf16[3,64,1152]{2,1,0:T(8,128)(2,1)} %get-tuple-element.61, bf16[3,64,1152]{2,1,0:T(8,128)(2,1)} %get-tuple-element.61, ...), branch_computations={%region_0.0_spmd, %region_1.0_spmd, %region_2.0_spmd, %region_3.0_... | conditional | flops 221184 | bytes 2949168 | solution.py:36
  50.9 1.1 slice.84
  52.0 5.4 %collective-permute-start.8 = (bf16[1,64,1152]{2,1,0:T(8,128)(2,1)S(1)}, bf16[1,64,1152]{2,1,0:T(8,128)(2,1)S(1)}, u32[]{:S(2)}, u32[]{:S(2)}) collective-permute-start(bf16[1,64,1152]{2,1,0:T(8,128)(2,1)S(1)} %slice.84), channel_id=1, source_target_pairs={{0,96},{24,120},{48,144},{72,168},{96,0},{120,24},{144,48},{168,72... | collective-permute-start | bytes 442376 | tf_op jit(solution)/shard_map/cond/branch_4_fun/ppermute | solution.py:24
  57.4 1.0 slice.85
  58.4 9.4 %collective-permute-done.8 = bf16[1,64,1152]{2,1,0:T(8,128)(2,1)S(1)} collective-permute-done((bf16[1,64,1152]{2,1,0:T(8,128)(2,1)S(1)}, bf16[1,64,1152]{2,1,0:T(8,128)(2,1)S(1)}, u32[]{:S(2)}, u32[]{:S(2)}) %collective-permute-start.8) | collective-permute-done | bytes 147488 | tf_op jit(solution)/shard_map/cond/branch_4_fun/ppermute | solution.py:24
  67.8 0.8 pad_maximum_fusion.2
  68.6 0.0 all-to-all-done
  68.6 0.0 collective-permute-done.21.other_pictures
  68.6 0.0 collective-permute-done.22.other_texts
  68.6 0.0 copy-done
  68.6 0.0 copy-done.1
  68.6 7.1 %shard_map.80 = (f32[8,64,1152]{2,1,0:T(8,128)S(1)}, f32[3,64,1152]{2,1,0:T(8,128)S(1)}) custom-call(s32[15]{0:T(128)S(1)} %get-tuple-element.58.info, f32[1]{0:T(128)S(6)} %copy.28.steepness, f32[1]{0:T(128)S(6)} %copy.29.shift, bf16[8,64,1152]{2,1,0:T(8,128)(2,1)} %bitcast.1.main, bf16[3,64,1152]{2,1,0:T(8,128)(2,1)} %get-tuple-element.84.rest, ...), custom_call_target="tpu_custom_call" | custom-call | tf_op jit(solution)/shard_map/pallas_call | solution.py:235
  75.7 0.0 copy-start.6
  75.7 1.3 convert_element_type.128
  77.0 4.3 %all-to-all-start.1 = ((f16[4,128,1152]{2,1,0:T(8,128)(2,1)}), f16[4,128,1152]{2,1,0:T(8,128)(2,1)}, u32[]{:S(2)}, u32[]{:S(2)}) async-start(f16[4,128,1152]{2,1,0:T(8,128)(2,1)} %bitcast.18), calls=%async_computation.1 | async-start | bytes 2359296 | tf_op jit(solution)/shard_map/all_to_all | solution.py:31
  81.3 0.6 copy-done.13
  81.9 0.6 slice.118
  82.4 0.6 slice.120
  83.0 0.7 slice.122
  83.7 0.6 slice.124
  84.3 2.0 %convert_element_type.131 = f16[3,64,1152]{2,1,0:T(8,128)(2,1)} convert(f32[3,64,1152]{2,1,0:T(8,128)} %copy-done.6) | non-fusion elementwise | flops 221184 | bytes 1327104 | tf_op jit(solution)/shard_map/convert_element_type | solution.py:256
  86.3 13.9 %conditional.3 = (f16[3,64,1152]{2,1,0:T(8,128)(2,1)}) conditional(s32[]{:T(128)} %bitcast.2, f16[3,64,1152]{2,1,0:T(8,128)(2,1)} %convert_element_type.131, f16[3,64,1152]{2,1,0:T(8,128)(2,1)} %convert_element_type.131, f16[3,64,1152]{2,1,0:T(8,128)(2,1)} %convert_element_type.131, ...), branch_computations={%region_11.0_spmd, %region_12.0_spmd, %region_13.0_spmd, %region_1... | conditional | flops 221184 | bytes 2949168 | solution.py:36
  86.3 0.9 slice.96
  87.2 5.4 %collective-permute-start.14 = (f16[1,64,1152]{2,1,0:T(8,128)(2,1)S(1)}, f16[1,64,1152]{2,1,0:T(8,128)(2,1)S(1)}, u32[]{:S(2)}, u32[]{:S(2)}) collective-permute-start(f16[1,64,1152]{2,1,0:T(8,128)(2,1)S(1)} %slice.96), channel_id=1, source_target_pairs={{0,96},{24,120},{48,144},{72,168},{96,0},{120,24},{144,48},{168,72... | collective-permute-start | bytes 442376 | tf_op jit(solution)/shard_map/cond/branch_4_fun/ppermute | solution.py:24
  92.6 1.0 slice.97
  93.6 5.7 %collective-permute-done.14 = f16[1,64,1152]{2,1,0:T(8,128)(2,1)S(1)} collective-permute-done((f16[1,64,1152]{2,1,0:T(8,128)(2,1)S(1)}, f16[1,64,1152]{2,1,0:T(8,128)(2,1)S(1)}, u32[]{:S(2)}, u32[]{:S(2)}) %collective-permute-start.14) | collective-permute-done | bytes 147488 | tf_op jit(solution)/shard_map/cond/branch_4_fun/ppermute | solution.py:24
  99.3 0.9 pad_maximum_fusion.8
  100.2 2.5 %fusion.4 = (f32[64,1152]{1,0:T(8,128)}, f32[64,1152]{1,0:T(8,128)}, f32[64,1152]{1,0:T(8,128)}, f32[64,1152]{1,0:T(8,128)}) fusion(f16[3,64,1152]{2,1,0:T(8,128)(2,1)} %get-tuple-element.85, pred[3]{0:T(512)(128)(4,1)} %slice.118, pred[3]{0:T(512)(128)(4,1)} %slice.120, pred[3]{0:T(512)(128)(4,1)} %slice.122, pred[3]{0:T(512)(128)(4,1)} %slice.124), kind=kLoop, calls=%fused_computation.24 | loop fusion | flops 1695744 | bytes 1622028 | tf_op jit(solution)/shard_map/reduce_sum | solution.py:262
  102.7 0.0 all-to-all-done.1
  102.8 2.5 %fusion = (f32[64,1152]{1,0:T(8,128)S(1)}, f32[64,1152]{1,0:T(8,128)S(1)}, f32[64,1152]{1,0:T(8,128)S(1)}, f32[64,1152]{1,0:T(8,128)S(1)}) fusion(f16[8,64,1152]{2,1,0:T(8,128)(2,1)} %bitcast.6, pred[8]{0:T(512)(128)(4,1)S(1)} %bitcast.22, pred[8]{0:T(512)(128)(4,1)S(1)} %bitcast.21, pred[8]{0:T(512)(128)(4,1)S(1)} %bitcast.20, pred[8]{0:T(512)(128)(4,1)S(1)} %bitcast.19), kind=kLoop, calls=%fused_computation.16 | loop fusion | flops 5013504 | bytes 2359328 | tf_op jit(solution)/shard_map/reduce_sum | solution.py:261
  105.3 0.1 fusion.8
  105.4 0.0 copy-done.8
  105.4 0.0 copy-done.9
  105.4 0.0 copy-start.12
  105.4 0.1 fusion.10
  105.5 1.0 pad_maximum_fusion.12
  106.5 10.4 %all-to-all-start.2 = ((f16[4,64,1152]{2,1,0:T(8,128)(2,1)}), f16[4,64,1152]{2,1,0:T(8,128)(2,1)}, u32[]{:S(2)}, u32[]{:S(2)}) async-start(f16[4,64,1152]{2,1,0:T(8,128)(2,1)} %pad_maximum_fusion.12), calls=%async_computation.2 | async-start | bytes 1179648 | tf_op jit(solution)/shard_map/all_to_all | solution.py:266
  116.9 0.0 copy-done.12
  117.0 0.0 copy-start.3
  117.0 0.9 copy-done.3
  117.9 2.2 %shard_map.77 = f32[64,1152]{1,0:T(8,128)S(1)} custom-call(f32[1]{0:T(128)S(6)} %copy.28.steepness, f32[1]{0:T(128)S(6)} %copy.29.shift, s32[1,768]{1,0:T(1,128)S(1)} %broadcast_in_dim.67.matched, bf16[64,1152]{1,0:T(8,128)(2,1)S(1)} %copy-done.3, bf16[768,1152]{1,0:T(8,128)(2,1)S(1)} %copy-done.1, bf16[768,1152]{1,0:T(8,128)(2,1)S(1)} %copy-done), custom_call_target="tpu_custom_call" | custom-call | tf_op jit(solution)/shard_map/pallas_call | solution.py:197
  120.1 0.7 copy-done.4
  120.8 21.9 %all-to-all-done.2 = f16[4,64,1152]{2,1,0:T(8,128)(2,1)} async-done(((f16[4,64,1152]{2,1,0:T(8,128)(2,1)}), f16[4,64,1152]{2,1,0:T(8,128)(2,1)}, u32[]{:S(2)}, u32[]{:S(2)}) %all-to-all-start.2) | async-done | bytes 589856 | tf_op jit(solution)/shard_map/all_to_all | solution.py:266
  142.7 1.2 convert_element_type.141
  143.8 0.1 slice_reduce_fusion
  143.9 0.7 slice_add_fusion
  (17 shorter events, 0.1 us)
Async XLA Ops:
  0.6 68.0 %collective-permute-start.21 = (bf16[768,1152]{1,0:T(8,128)(2,1)}, bf16[768,1152]{1,0:T(8,128)(2,1)}, u32[]{:S(2)}, u32[]{:S(2)}) collective-permute-start(bf16[768,1152]{1,0:T(8,128)(2,1)} %pictures.3), channel_id=1, source_target_pairs={{0,24},{24,0},{48,72},{72,48},{96,120},{120,96},{144,168},{168,144... | collective-permute-start | bytes 5308424 | tf_op jit(solution)/shard_map/ppermute | solution.py:187
  2.6 66.0 %collective-permute-start.22 = (bf16[768,1152]{1,0:T(8,128)(2,1)}, bf16[768,1152]{1,0:T(8,128)(2,1)}, u32[]{:S(2)}, u32[]{:S(2)}) collective-permute-start(bf16[768,1152]{1,0:T(8,128)(2,1)} %texts.3), channel_id=1, source_target_pairs={{0,24},{24,0},{48,72},{72,48},{96,120},{120,96},{144,168},{168,144... | collective-permute-start | bytes 5308424 | tf_op jit(solution)/shard_map/ppermute | solution.py:188
  6.8 23.4 %collective-permute-start.18 = (bf16[64,1152]{1,0:T(8,128)(2,1)S(1)}, bf16[64,1152]{1,0:T(8,128)(2,1)S(1)}, u32[]{:S(2)}, u32[]{:S(2)}) collective-permute-start(bf16[64,1152]{1,0:T(8,128)(2,1)S(1)} %pad_maximum_fusion.13.shares.refs_0_), channel_id=1, source_target_pairs={{0,192},{24,216},{48,240},{72,264},{96,288},{120,312},{144,336},{1... | collective-permute-start | bytes 442376 | tf_op jit(solution)/shard_map/ppermute | solution.py:196
  15.9 23.9 %collective-permute-start.19 = (bf16[64,1152]{1,0:T(8,128)(2,1)S(1)}, bf16[64,1152]{1,0:T(8,128)(2,1)S(1)}, u32[]{:S(2)}, u32[]{:S(2)}) collective-permute-start(bf16[64,1152]{1,0:T(8,128)(2,1)S(1)} %pad_maximum_fusion.13.shares.refs_0_), channel_id=1, source_target_pairs={{0,384},{24,408},{48,432},{72,456},{96,480},{120,504},{144,528},{1... | collective-permute-start | bytes 442376 | tf_op jit(solution)/shard_map/ppermute | solution.py:196
  26.2 15.5 %collective-permute-start.20 = (bf16[64,1152]{1,0:T(8,128)(2,1)S(1)}, bf16[64,1152]{1,0:T(8,128)(2,1)S(1)}, u32[]{:S(2)}, u32[]{:S(2)}) collective-permute-start(bf16[64,1152]{1,0:T(8,128)(2,1)S(1)} %pad_maximum_fusion.13.shares.refs_0_), channel_id=1, source_target_pairs={{0,576},{24,600},{48,624},{72,648},{96,672},{120,696},{144,720},{1... | collective-permute-start | bytes 442376 | tf_op jit(solution)/shard_map/ppermute | solution.py:196
  28.2 0.7 copy-start.7
  43.9 0.7 copy-start.2
  44.6 24.0 %all-to-all-start = ((bf16[4,128,1152]{2,1,0:T(8,128)(2,1)}), bf16[4,128,1152]{2,1,0:T(8,128)(2,1)}, u32[]{:S(2)}, u32[]{:S(2)}) async-start(bf16[4,128,1152]{2,1,0:T(8,128)(2,1)} %bitcast), calls=%async_computation | async-start | bytes 2359296 | tf_op jit(solution)/shard_map/all_to_all | solution.py:31
  50.8 17.8 %copy-start = (bf16[768,1152]{1,0:T(8,128)(2,1)S(1)}, bf16[768,1152]{1,0:T(8,128)(2,1)}, u32[]{:S(2)}) copy-start(bf16[768,1152]{1,0:T(8,128)(2,1)} %texts.3) | copy-start | bytes 5308420
  50.8 17.8 %copy-start.1 = (bf16[768,1152]{1,0:T(8,128)(2,1)S(1)}, bf16[768,1152]{1,0:T(8,128)(2,1)}, u32[]{:S(2)}) copy-start(bf16[768,1152]{1,0:T(8,128)(2,1)} %pictures.3) | copy-start | bytes 5308420
  52.0 15.8 %collective-permute-start.8 = (bf16[1,64,1152]{2,1,0:T(8,128)(2,1)S(1)}, bf16[1,64,1152]{2,1,0:T(8,128)(2,1)S(1)}, u32[]{:S(2)}, u32[]{:S(2)}) collective-permute-start(bf16[1,64,1152]{2,1,0:T(8,128)(2,1)S(1)} %slice.84), channel_id=1, source_target_pairs={{0,96},{24,120},{48,144},{72,168},{96,0},{120,24},{144,48},{168,72... | collective-permute-start | bytes 442376 | tf_op jit(solution)/shard_map/cond/branch_4_fun/ppermute | solution.py:24
  75.7 1.3 copy-start.6
  77.0 25.7 %all-to-all-start.1 = ((f16[4,128,1152]{2,1,0:T(8,128)(2,1)}), f16[4,128,1152]{2,1,0:T(8,128)(2,1)}, u32[]{:S(2)}, u32[]{:S(2)}) async-start(f16[4,128,1152]{2,1,0:T(8,128)(2,1)} %bitcast.18), calls=%async_computation.1 | async-start | bytes 2359296 | tf_op jit(solution)/shard_map/all_to_all | solution.py:31
  81.3 0.6 copy-start.13
  86.3 16.4 %copy-start.14 = (pred[11]{0:T(512)(128)(4,1)S(1)}, pred[11]{0:T(512)(128)(4,1)}, u32[]{:S(2)}) copy-start(pred[11]{0:T(512)(128)(4,1)} %copy-done.13) | copy-start | bytes 37
  87.2 12.1 %collective-permute-start.14 = (f16[1,64,1152]{2,1,0:T(8,128)(2,1)S(1)}, f16[1,64,1152]{2,1,0:T(8,128)(2,1)S(1)}, u32[]{:S(2)}, u32[]{:S(2)}) collective-permute-start(f16[1,64,1152]{2,1,0:T(8,128)(2,1)S(1)} %slice.96), channel_id=1, source_target_pairs={{0,96},{24,120},{48,144},{72,168},{96,0},{120,24},{144,48},{168,72... | collective-permute-start | bytes 442376 | tf_op jit(solution)/shard_map/cond/branch_4_fun/ppermute | solution.py:24
  102.7 2.6 %copy-start.10 = (f32[64,1152]{1,0:T(8,128)S(1)}, f32[64,1152]{1,0:T(8,128)}, u32[]{:S(2)}) copy-start(f32[64,1152]{1,0:T(8,128)} %get-tuple-element.70) | copy-start | bytes 884740
  102.7 2.6 %copy-start.11 = (f32[64,1152]{1,0:T(8,128)S(1)}, f32[64,1152]{1,0:T(8,128)}, u32[]{:S(2)}) copy-start(f32[64,1152]{1,0:T(8,128)} %get-tuple-element.71) | copy-start | bytes 884740
  102.7 2.6 %copy-start.8 = (f32[64,1152]{1,0:T(8,128)S(1)}, f32[64,1152]{1,0:T(8,128)}, u32[]{:S(2)}) copy-start(f32[64,1152]{1,0:T(8,128)} %get-tuple-element.72) | copy-start | bytes 884740
  102.8 2.6 %copy-start.9 = (f32[64,1152]{1,0:T(8,128)S(1)}, f32[64,1152]{1,0:T(8,128)}, u32[]{:S(2)}) copy-start(f32[64,1152]{1,0:T(8,128)} %get-tuple-element.73) | copy-start | bytes 884740
  105.4 11.5 %copy-start.12 = (s32[768]{0:T(1024)S(1)}, s32[768]{0:T(1024)}, u32[]{:S(2)}) copy-start(s32[768]{0:T(1024)} %param.28) | copy-start | bytes 9220
  106.5 36.2 %all-to-all-start.2 = ((f16[4,64,1152]{2,1,0:T(8,128)(2,1)}), f16[4,64,1152]{2,1,0:T(8,128)(2,1)}, u32[]{:S(2)}, u32[]{:S(2)}) async-start(f16[4,64,1152]{2,1,0:T(8,128)(2,1)} %pad_maximum_fusion.12), calls=%async_computation.2 | async-start | bytes 1179648 | tf_op jit(solution)/shard_map/all_to_all | solution.py:266
  117.0 0.9 copy-start.3
  120.1 0.7 copy-start.4
  142.7 1.3 copy-start.5

commit v3 on v2

v3 whole, which is shorter than its diff:
```python
import functools
import jax
import jax.numpy as jnp
from jax import lax
from jax.experimental import pallas as pl
from jax.experimental.pallas import tpu as pltpu
from jax.sharding import PartitionSpec as P

WIDE = 32
Z_SETS = [[low + 8 * z for z in range(4)] for low in range(8)]
X_SETS = [[8 * z + 2 * x + core for x in range(4)] for z in range(4) for core in range(2)]
CAP = 2
MAIN = 4 * CAP
PICK_VMEM = 8 * 1024 * 1024
GRAD_VMEM = 24 * 1024 * 1024


def xor_pairs(mask):
    return [(i, i ^ mask) for i in range(WIDE)]


def move_spare(mask, count, stack):
    moved = lax.ppermute(stack[:count], "wide", xor_pairs(2 * mask))
    return jnp.concatenate([moved, stack[count:]], axis=0) if count < stack.shape[0] else moved


def exchange_x(spare, main, rest):
    places, tall, span = main.shape
    moves = [lambda stack: stack]
    for mask in (1, 2, 3):
        for count in range(1, rest.shape[0] + 1):
            moves.append(functools.partial(move_spare, mask, count))
    main, rest = lax.optimization_barrier((main, lax.switch(spare, moves, rest)))
    sent = main.reshape(4, CAP * tall, span)
    main = lax.all_to_all(sent, "wide", 0, 0, axis_index_groups=X_SETS).reshape(places, tall, span)
    return lax.optimization_barrier((main, rest))


def pick_kernel(rounds, table, gathered, main, rest, spare, info, homes):
    my_z = lax.axis_index("wide") // 8
    my_x = (lax.axis_index("wide") // 2) % 4
    masks = [table[r, 0] & (WIDE - 1) for r in range(rounds)]
    x_masks = [(mask >> 1) & 3 for mask in masks]
    for place in range(MAIN + rounds - CAP):
        homes[place] = -1
    main[...] = jnp.zeros_like(main)
    rest[...] = jnp.zeros_like(rest)
    beyond = jnp.int32(0)
    index = jnp.int32(0)
    for r in range(rounds):
        before = sum([(x_masks[s] == x_masks[r]).astype(jnp.int32) for s in range(r)], jnp.int32(0))
        fits = before < CAP
        place = jnp.where(fits, (my_x ^ x_masks[r]) * CAP + before, MAIN + beyond)
        beyond += jnp.where(fits, 0, 1)
        over = before - CAP + 1
        index = jnp.where(fits | (x_masks[r] == 0), index, (x_masks[r] - 1) * (rounds - CAP) + over)
        home = my_z ^ (masks[r] >> 3)
        info[r] = masks[r] & 1
        info[rounds + r] = place
        homes[place] = home

        @pl.when(place < MAIN)
        def _():
            main[place] = gathered[home]

        @pl.when(place >= MAIN)
        def _():
            rest[place - MAIN] = gathered[home]

    spare[0] = index


def dot_last(left, right):
    return lax.dot_general(left, right, (((1,), (1,)), ((), ())), preferred_element_type=jnp.float32)


def dot(left, right):
    return jnp.dot(left, right, preferred_element_type=jnp.float32)


def grad_kernel(
    rounds,
    info,
    steepness,
    shift,
    matched,
    shares,
    main,
    rest,
    pictures,
    texts,
    other_pictures,
    other_texts,
    back_main,
    back_rest,
    own,
    left,
):
    rows, span = pictures.shape
    share = main.shape[1] // 2
    first = lax.axis_index("wide") * rows
    begin = lax.axis_index("narrow") * share
    scale = steepness[0] / span
    bias = shift[0]
    lanes = lax.broadcasted_iota(jnp.int32, (share, rows), 1)
    mine = begin + lax.broadcasted_iota(jnp.int32, (share, rows), 0)
    matches = jnp.broadcast_to(matched[...], (share, rows))
    my_match = jnp.sum(jnp.where(lanes == mine, matches, 0), axis=1, keepdims=True)
    back_main[...] = jnp.zeros_like(back_main)
    back_rest[...] = jnp.zeros_like(back_rest)
    for kind in range(2):
        kind_rows = slice(kind * share, (kind + 1) * share)
        left[kind, rounds * share :, :] = shares[kind_rows, :]
        for r in range(rounds):
            place = info[rounds + r]
            left_rows = slice(r * share, (r + 1) * share)

            @pl.when(place < MAIN)
            def _():
                left[kind, left_rows, :] = main[place, kind_rows, :]

            @pl.when(place >= MAIN)
            def _():
                left[kind, left_rows, :] = rest[place - MAIN, kind_rows, :]

    for kind, (block, other) in enumerate([(texts, other_texts), (pictures, other_pictures)]):
        kind_rows = slice(kind * share, (kind + 1) * share)
        near = dot_last(left[kind], block[...])
        far = dot_last(left[kind, : rounds * share, :], other[...])
        near_weights = []
        far_weights = []
        for r in range(rounds):
            apart = info[r] == 1
            left_rows = slice(r * share, (r + 1) * share)
            products = jnp.where(apart, far[left_rows], near[left_rows])
            weights = scale * jax.nn.sigmoid(scale * products + bias)
            near_weights.append(jnp.where(apart, 0.0, weights).astype(jnp.bfloat16))
            far_weights.append(jnp.where(apart, weights, 0.0).astype(jnp.bfloat16))
        same = (my_match == first + lanes) if kind == 0 else (matches == first + mine)
        signs = jnp.where(same, 1.0, -1.0).astype(jnp.float32)
        logits = scale * near[rounds * share :] + bias
        near_weights.append((-scale * signs * jax.nn.sigmoid(-signs * logits)).astype(jnp.bfloat16))
        near_slopes = dot(jnp.concatenate(near_weights, axis=0), block[...])
        slopes = near_slopes[: rounds * share] + dot(jnp.concatenate(far_weights, axis=0), other[...])
        own[kind_rows, :] = near_slopes[rounds * share :]
        for r in range(rounds):
            place = info[rounds + r]
            slope = slopes[r * share : (r + 1) * share]

            @pl.when(place < MAIN)
            def _():
                back_main[place, kind_rows, :] = slope

            @pl.when(place >= MAIN)
            def _():
                back_rest[place - MAIN, kind_rows, :] = slope


def local(
    picture_vectors,
    sentence_vectors,
    matched_text_indices,
    partner_table,
    trained_steepness,
    learned_shift,
):
    rows, span = picture_vectors.shape
    rounds = partner_table.shape[0]
    share = rows // lax.axis_size("narrow")
    begin = lax.axis_index("narrow") * share
    smem = pl.BlockSpec(memory_space=pltpu.SMEM)
    vmem = pl.BlockSpec(memory_space=pltpu.VMEM)

    other_pictures = lax.ppermute(picture_vectors, "wide", xor_pairs(1))
    other_texts = lax.ppermute(sentence_vectors, "wide", xor_pairs(1))
    shares = jnp.concatenate(
        [
            lax.dynamic_slice_in_dim(picture_vectors, begin, share, 0),
            lax.dynamic_slice_in_dim(sentence_vectors, begin, share, 0),
        ],
        axis=0,
    )
    gathered = lax.all_gather(shares, "wide", axis_index_groups=Z_SETS)
    main_shape = (MAIN, 2 * share, span)
    rest_shape = (rounds - CAP, 2 * share, span)
    main, rest, spare, info, homes = pl.pallas_call(
        functools.partial(pick_kernel, rounds),
        out_shape=[
            jax.ShapeDtypeStruct(main_shape, jnp.bfloat16),
            jax.ShapeDtypeStruct(rest_shape, jnp.bfloat16),
            jax.ShapeDtypeStruct((1,), jnp.int32),
            jax.ShapeDtypeStruct((2 * rounds,), jnp.int32),
            jax.ShapeDtypeStruct((MAIN + rounds - CAP,), jnp.int32),
        ],
        in_specs=[smem, vmem],
        out_specs=[vmem, vmem, smem, smem, smem],
        compiler_params=pltpu.CompilerParams(vmem_limit_bytes=PICK_VMEM),
    )(partner_table, gathered)
    main, rest = exchange_x(spare[0], main, rest)
    main, rest, own = pl.pallas_call(
        functools.partial(grad_kernel, rounds),
        out_shape=[
            jax.ShapeDtypeStruct(main_shape, jnp.float32),
            jax.ShapeDtypeStruct(rest_shape, jnp.float32),
            jax.ShapeDtypeStruct((2 * share, span), jnp.float32),
        ],
        in_specs=[smem, smem, smem] + [vmem] * 8,
        out_specs=[vmem, vmem, vmem],
        scratch_shapes=[pltpu.VMEM((2, (rounds + 1) * share, span), jnp.bfloat16)],
        compiler_params=pltpu.CompilerParams(vmem_limit_bytes=GRAD_VMEM),
    )(
        info,
        trained_steepness,
        learned_shift,
        matched_text_indices[None, :],
        shares,
        main,
        rest,
        picture_vectors,
        sentence_vectors,
        other_pictures,
        other_texts,
    )
    main, rest = exchange_x(spare[0], main.astype(jnp.float16), rest.astype(jnp.float16))
    main, homes = lax.optimization_barrier((main, homes))

    def by_home(stack, places):
        chosen = places[None, :] == jnp.arange(4, dtype=jnp.int32)[:, None]
        return jnp.sum(jnp.where(chosen[:, :, None, None], stack[None].astype(jnp.float32), 0.0), axis=1)

    sums = (by_home(main, homes[:MAIN]) + by_home(rest, homes[MAIN:])).astype(jnp.float16)
    arrived = lax.all_to_all(sums, "wide", 0, 0, axis_index_groups=Z_SETS)
    arrived, own = lax.optimization_barrier((arrived, own))
    slopes = own + jnp.sum(arrived.astype(jnp.float32), axis=0)
    return slopes[:share], slopes[share:]


def solution(mesh):
    in_specs = (P("wide", None), P("wide", None), P("wide"), P(), P(), P())
    out_specs = (P(("wide", "narrow"), None), P(("wide", "narrow"), None))
    return jax.shard_map(local, mesh=mesh, in_specs=in_specs, out_specs=out_specs, check_vma=False)
```

time: 146 us -> 136 us (0.932)
  blocking collectives: 0 us -> 70.9 us
  starting transfers between devices: 55.5 us -> 16.2 us
  waiting for transfers between devices: 48.5 us -> 27.3 us
  other arithmetic: 13.2 us -> 3 us
  local copies, waits for them, and re-layouts: 11.8 us -> 6.92 us
  Pallas kernels: 12.7 us -> 8.49 us
    all_to_all x0 -> x2, blocking collectives: none -> 39.2 us  [the longest x1 23.2 us: local(): arrived = lax.all_to_all(sums, 'wide', 0, 0, axis_index_groups=Z_SETS)]
    all_gather x0 -> x1, blocking collectives: none -> 31.8 us  [local(): gathered = lax.all_gather(shares, 'wide', axis_index_groups=Z_SETS)]
    all_to_all x1 -> x0, waiting for transfers between devices: 21.9 us -> none  [local(): arrived = lax.all_to_all(sums, 'wide', 0, 0, axis_index_groups=Z_SETS)]
    ppermute x3 -> x0, starting transfers between devices: 21.4 us -> none  [local(): lax.ppermute(shares, 'wide', xor_pairs(8 * mask))]
    all_to_all x2 -> x1, waiting for transfers between devices: 0.01 us -> 14.3 us  [exchange_x(): lax.all_to_all(sent, 'wide', 0, 0, axis_index_groups=X_SETS)]
    ppermute x3 -> x0, waiting for transfers between devices: 11.6 us -> none  [local(): lax.ppermute(shares, 'wide', xor_pairs(8 * mask))]
    all_to_all x1 -> x0, starting transfers between devices: 10.4 us -> none  [local(): arrived = lax.all_to_all(sums, 'wide', 0, 0, axis_index_groups=Z_SETS)]
    all_to_all x2 -> x1, starting transfers between devices: 8.56 us -> 4.11 us  [exchange_x(): lax.all_to_all(sent, 'wide', 0, 0, axis_index_groups=X_SETS)]
  transfers between devices with their start and end apart: 10 -> 5, of which waited for: 5 -> 3; matrix products, arithmetic and copies ran while one was open for 10% -> 3% of each run, Pallas kernels for 4% -> 1%
where the time goes in v3:
time: 136 us
  blocking collectives  70.9 us (52%)
  waiting for transfers between devices  27.3 us (20%)
  starting transfers between devices  16.2 us (12%)
  Pallas kernels  8.49 us (6%)
  local copies, waits for them, and re-layouts  6.92 us (5%)
  other arithmetic  3 us (2%)
  between operations  2.75 us (2%)
    all_gather x1, blocking collectives, local(): gathered = lax.all_gather(shares, 'wide', axis_index_groups=Z_SETS)  31.8 us
    all_to_all x1, blocking collectives, local(): arrived = lax.all_to_all(sums, 'wide', 0, 0, axis_index_groups=Z_SETS)  23.2 us
    all_to_all x1, blocking collectives, exchange_x(): lax.all_to_all(sent, 'wide', 0, 0, axis_index_groups=X_SETS)  16 us
    all_to_all x1, waiting for transfers between devices, exchange_x(): lax.all_to_all(sent, 'wide', 0, 0, axis_index_groups=X_SETS)  14.3 us
    ppermute x2, waiting for transfers between devices, move_spare(): moved = lax.ppermute(stack[:count], 'wide', xor_pairs(2 * mask))  13 us
    ppermute x2, starting transfers between devices, move_spare(): moved = lax.ppermute(stack[:count], 'wide', xor_pairs(2 * mask))  7.76 us
    pallas_call x1, Pallas kernels, local(): pl.pallas_call(functools.partial(grad_kernel, rounds), out_shape=[jax.Sha...  6.87 us
    all_to_all x1, starting transfers between devices, exchange_x(): lax.all_to_all(sent, 'wide', 0, 0, axis_index_groups=X_SETS)  4.11 us
  transfers between devices with their start and end apart: 5, of which 3 were waited for; matrix products, arithmetic and copies ran while one was open for 3% of the time, Pallas kernels for 1%

profile of v3, /device:TPU:64, one launch (start us, length us, event | category | flops | bytes accessed | tf_op | source)
XLA Modules:
  0.0 135.8 jit_solution(4970092202485180894)
XLA Ops:
  0.6 1.9 %collective-permute-start.18 = (bf16[768,1152]{1,0:T(8,128)(2,1)}, bf16[768,1152]{1,0:T(8,128)(2,1)}, u32[]{:S(2)}, u32[]{:S(2)}) collective-permute-start(bf16[768,1152]{1,0:T(8,128)(2,1)} %pictures.1), channel_id=1, source_target_pairs={{0,24},{24,0},{48,72},{72,48},{96,120},{120,96},{144,168},{168,144... | collective-permute-start | bytes 5308424 | tf_op jit(solution)/shard_map/ppermute | solution.py:174
  2.6 2.4 %collective-permute-start.19 = (bf16[768,1152]{1,0:T(8,128)(2,1)}, bf16[768,1152]{1,0:T(8,128)(2,1)}, u32[]{:S(2)}, u32[]{:S(2)}) collective-permute-start(bf16[768,1152]{1,0:T(8,128)(2,1)} %texts.1), channel_id=1, source_target_pairs={{0,24},{24,0},{48,72},{72,48},{96,120},{120,96},{144,168},{168,144... | collective-permute-start | bytes 5308424 | tf_op jit(solution)/shard_map/ppermute | solution.py:175
  5.0 0.9 constant_dynamic-slice_fusion
  6.0 31.8 %all-gather = bf16[256,1152]{1,0:T(8,128)(2,1)S(1)} all-gather(bf16[64,1152]{1,0:T(8,128)(2,1)S(1)} %pad_maximum_fusion.12.shares), channel_id=2, replica_groups={{0,192,384,576},{24,216,408,600},{48,240,432,624},{72,264,456,648},{96,..., dimensions={0}, use_global_device_ids=true | all-gather | bytes 737280 | tf_op jit(solution)/shard_map/all_gather | solution.py:183
  37.7 0.0 copy-start.3
  37.7 0.7 copy-done.3
  38.4 1.6 %shard_map.77 = (bf16[8,64,1152]{2,1,0:T(8,128)(2,1)S(1)}, bf16[3,64,1152]{2,1,0:T(8,128)(2,1)}, s32[1]{0:T(128)}, s32[10]{0:T(128)S(1)}, s32[11]{0:T(128)S(1)}) custom-call(s32[5,32]{1,0:T(8,128)S(1)} %copy-done.3, bf16[4,64,1152]{2,1,0:T(8,128)(2,1)S(1)} %bitcast.8), custom_call_target="tpu_custom_call" | custom-call | tf_op jit(solution)/shard_map/pallas_call | solution.py:186
  40.0 0.0 copy-start.2
  40.1 1.0 copy-done.2
  41.7 13.8 %conditional.2 = (bf16[3,64,1152]{2,1,0:T(8,128)(2,1)}) conditional(s32[]{:T(128)} %bitcast.1, bf16[3,64,1152]{2,1,0:T(8,128)(2,1)} %get-tuple-element.67, bf16[3,64,1152]{2,1,0:T(8,128)(2,1)} %get-tuple-element.67, bf16[3,64,1152]{2,1,0:T(8,128)(2,1)} %get-tuple-element.67, ...), branch_computations={%region_0.0_spmd, %region_1.0_spmd, %region_2.0_spmd, %region_3.0_... | conditional | flops 221184 | bytes 2949168 | solution.py:33
  41.8 1.0 slice.66
  42.8 4.7 %collective-permute-start.11 = (bf16[2,64,1152]{2,1,0:T(8,128)(2,1)S(1)}, bf16[2,64,1152]{2,1,0:T(8,128)(2,1)S(1)}, u32[]{:S(2)}, u32[]{:S(2)}) collective-permute-start(bf16[2,64,1152]{2,1,0:T(8,128)(2,1)S(1)} %slice.66), channel_id=1, source_target_pairs={{0,144},{24,168},{48,96},{72,120},{96,48},{120,72},{144,0},{168,24... | collective-permute-start | bytes 884744 | tf_op jit(solution)/shard_map/cond/branch_8_fun/ppermute | solution.py:23
  47.5 0.9 slice.67
  48.4 6.3 %collective-permute-done.11 = bf16[2,64,1152]{2,1,0:T(8,128)(2,1)S(1)} collective-permute-done((bf16[2,64,1152]{2,1,0:T(8,128)(2,1)S(1)}, bf16[2,64,1152]{2,1,0:T(8,128)(2,1)S(1)}, u32[]{:S(2)}, u32[]{:S(2)}) %collective-permute-start.11) | collective-permute-done | bytes 294944 | tf_op jit(solution)/shard_map/cond/branch_8_fun/ppermute | solution.py:23
  54.7 0.8 pad_maximum_fusion.5
  55.5 0.0 copy-start.4
  55.5 0.0 copy-start
  55.5 4.1 %all-to-all-start = ((bf16[4,128,1152]{2,1,0:T(8,128)(2,1)}), bf16[4,128,1152]{2,1,0:T(8,128)(2,1)S(1)}, u32[]{:S(2)}, u32[]{:S(2)}) async-start(bf16[4,128,1152]{2,1,0:T(8,128)(2,1)} %bitcast.9), calls=%async_computation | async-start | bytes 2359296 | tf_op jit(solution)/shard_map/all_to_all | solution.py:35
  60.9 0.0 copy-done.4
  61.0 14.3 %all-to-all-done = bf16[4,128,1152]{2,1,0:T(8,128)(2,1)S(1)} async-done(((bf16[4,128,1152]{2,1,0:T(8,128)(2,1)}), bf16[4,128,1152]{2,1,0:T(8,128)(2,1)S(1)}, u32[]{:S(2)}, u32[]{:S(2)}) %all-to-all-start) | async-done | bytes 1179680 | tf_op jit(solution)/shard_map/all_to_all | solution.py:35
  75.3 0.0 collective-permute-done.18.other_pictures
  75.3 0.0 collective-permute-done.19.other_texts
  75.3 0.0 copy-done
  75.3 0.0 copy-start.1
  75.3 1.5 %copy-done.1 = bf16[768,1152]{1,0:T(8,128)(2,1)S(1)} copy-done((bf16[768,1152]{1,0:T(8,128)(2,1)S(1)}, bf16[768,1152]{1,0:T(8,128)(2,1)}, u32[]{:S(2)}) %copy-start.1) | copy-done | bytes 1769496
  76.8 6.9 %shard_map.78 = (f32[8,64,1152]{2,1,0:T(8,128)S(1)}, f32[3,64,1152]{2,1,0:T(8,128)S(1)}, f32[64,1152]{1,0:T(8,128)S(1)}) custom-call(s32[10]{0:T(128)S(1)} %get-tuple-element.64.info, f32[1]{0:T(128)S(6)} %copy.28.steepness, f32[1]{0:T(128)S(6)} %copy.29.shift, s32[1,768]{1,0:T(1,128)S(1)} %broadcast_in_dim.51.matched, ...), custom_call_target="tpu_custom_call" | custom-call | tf_op jit(solution)/shard_map/pallas_call | solution.py:200
  83.6 0.2 convert_element_type.50
  83.8 0.1 convert_element_type.51
  83.9 10.1 %conditional.3 = (f16[3,64,1152]{2,1,0:T(8,128)(2,1)S(1)}) conditional(s32[]{:T(128)} %bitcast.1, f16[3,64,1152]{2,1,0:T(8,128)(2,1)S(1)} %convert_element_type.51, f16[3,64,1152]{2,1,0:T(8,128)(2,1)S(1)} %convert_element_type.51, f16[3,64,1152]{2,1,0:T(8,128)(2,1)S(1)} %convert_element_type.51, ...), branch_computations={%region_10.0_spmd, %region_11.0_spmd, %region_12.0_spmd, %region_1... | conditional | flops 221184 | bytes 2949168 | solution.py:33
  83.9 0.1 slice.78
  84.0 3.1 %collective-permute-start.17 = (f16[2,64,1152]{2,1,0:T(8,128)(2,1)S(1)}, f16[2,64,1152]{2,1,0:T(8,128)(2,1)S(1)}, u32[]{:S(2)}, u32[]{:S(2)}) collective-permute-start(f16[2,64,1152]{2,1,0:T(8,128)(2,1)S(1)} %slice.78), channel_id=1, source_target_pairs={{0,144},{24,168},{48,96},{72,120},{96,48},{120,72},{144,0},{168,24... | collective-permute-start | bytes 884744 | tf_op jit(solution)/shard_map/cond/branch_8_fun/ppermute | solution.py:23
  87.1 6.7 %collective-permute-done.17 = f16[2,64,1152]{2,1,0:T(8,128)(2,1)S(1)} collective-permute-done((f16[2,64,1152]{2,1,0:T(8,128)(2,1)S(1)}, f16[2,64,1152]{2,1,0:T(8,128)(2,1)S(1)}, u32[]{:S(2)}, u32[]{:S(2)}) %collective-permute-start.17) | collective-permute-done | bytes 294944 | tf_op jit(solution)/shard_map/cond/branch_8_fun/ppermute | solution.py:23
  93.8 0.1 pad_maximum_fusion.11
  93.9 16.0 %all_to_all.15 = f16[4,128,1152]{2,1,0:T(8,128)(2,1)S(1)} all-to-all(f16[4,128,1152]{2,1,0:T(8,128)(2,1)S(1)} %bitcast.11), channel_id=1, replica_groups={{0,48,96,144},{24,72,120,168},{192,240,288,336},{216,264,312,360},{384,..., dimensions={0} | all-to-all | bytes 2359296 | tf_op jit(solution)/shard_map/all_to_all | solution.py:35
  109.9 0.1 slice.85
  110.0 0.1 convert_element_type.53
  110.1 0.2 convert_element_type.52
  110.3 0.3 select_reduce_fusion.1
  110.6 1.0 select_reduce_fusion
  111.6 0.1 add_convert_fusion
  111.8 23.2 %all_to_all.16 = f16[4,64,1152]{2,1,0:T(8,128)(2,1)S(1)} all-to-all(f16[4,64,1152]{2,1,0:T(8,128)(2,1)S(1)} %add_convert_fusion), channel_id=1, replica_groups={{0,192,384,576},{24,216,408,600},{48,240,432,624},{72,264,456,648},{96,..., dimensions={0} | all-to-all | bytes 1179648 | tf_op jit(solution)/shard_map/all_to_all | solution.py:232
  134.9 0.1 convert_reduce_fusion
  135.1 0.7 fusion
  (6 shorter events, 0.1 us)
Async XLA Ops:
  0.6 74.6 %collective-permute-start.18 = (bf16[768,1152]{1,0:T(8,128)(2,1)}, bf16[768,1152]{1,0:T(8,128)(2,1)}, u32[]{:S(2)}, u32[]{:S(2)}) collective-permute-start(bf16[768,1152]{1,0:T(8,128)(2,1)} %pictures.1), channel_id=1, source_target_pairs={{0,24},{24,0},{48,72},{72,48},{96,120},{120,96},{144,168},{168,144... | collective-permute-start | bytes 5308424 | tf_op jit(solution)/shard_map/ppermute | solution.py:174
  2.6 72.7 %collective-permute-start.19 = (bf16[768,1152]{1,0:T(8,128)(2,1)}, bf16[768,1152]{1,0:T(8,128)(2,1)}, u32[]{:S(2)}, u32[]{:S(2)}) collective-permute-start(bf16[768,1152]{1,0:T(8,128)(2,1)} %texts.1), channel_id=1, source_target_pairs={{0,24},{24,0},{48,72},{72,48},{96,120},{120,96},{144,168},{168,144... | collective-permute-start | bytes 5308424 | tf_op jit(solution)/shard_map/ppermute | solution.py:175
  37.7 0.7 copy-start.3
  40.0 1.0 copy-start.2
  42.8 11.9 %collective-permute-start.11 = (bf16[2,64,1152]{2,1,0:T(8,128)(2,1)S(1)}, bf16[2,64,1152]{2,1,0:T(8,128)(2,1)S(1)}, u32[]{:S(2)}, u32[]{:S(2)}) collective-permute-start(bf16[2,64,1152]{2,1,0:T(8,128)(2,1)S(1)} %slice.66), channel_id=1, source_target_pairs={{0,144},{24,168},{48,96},{72,120},{96,48},{120,72},{144,0},{168,24... | collective-permute-start | bytes 884744 | tf_op jit(solution)/shard_map/cond/branch_8_fun/ppermute | solution.py:23
  55.5 5.4 %copy-start.4 = (s32[768]{0:T(1024)S(1)}, s32[768]{0:T(1024)}, u32[]{:S(2)}) copy-start(s32[768]{0:T(1024)} %param.28) | copy-start | bytes 9220
  55.5 19.8 %copy-start = (bf16[768,1152]{1,0:T(8,128)(2,1)S(1)}, bf16[768,1152]{1,0:T(8,128)(2,1)}, u32[]{:S(2)}) copy-start(bf16[768,1152]{1,0:T(8,128)(2,1)} %texts.1) | copy-start | bytes 5308420
  55.5 19.7 %all-to-all-start = ((bf16[4,128,1152]{2,1,0:T(8,128)(2,1)}), bf16[4,128,1152]{2,1,0:T(8,128)(2,1)S(1)}, u32[]{:S(2)}, u32[]{:S(2)}) async-start(bf16[4,128,1152]{2,1,0:T(8,128)(2,1)} %bitcast.9), calls=%async_computation | async-start | bytes 2359296 | tf_op jit(solution)/shard_map/all_to_all | solution.py:35
  75.3 1.5 %copy-start.1 = (bf16[768,1152]{1,0:T(8,128)(2,1)S(1)}, bf16[768,1152]{1,0:T(8,128)(2,1)}, u32[]{:S(2)}) copy-start(bf16[768,1152]{1,0:T(8,128)(2,1)} %pictures.1) | copy-start | bytes 5308420
  84.0 9.8 %collective-permute-start.17 = (f16[2,64,1152]{2,1,0:T(8,128)(2,1)S(1)}, f16[2,64,1152]{2,1,0:T(8,128)(2,1)S(1)}, u32[]{:S(2)}, u32[]{:S(2)}) collective-permute-start(f16[2,64,1152]{2,1,0:T(8,128)(2,1)S(1)} %slice.78), channel_id=1, source_target_pairs={{0,144},{24,168},{48,96},{72,120},{96,48},{120,72},{144,0},{168,24... | collective-permute-start | bytes 884744 | tf_op jit(solution)/shard_map/cond/branch_8_fun/ppermute | solution.py:23

commit v4 on v3

--- a/solution.py
+++ b/solution.py
@@ -24,13 +24,15 @@
     return jnp.concatenate([moved, stack[count:]], axis=0) if count < stack.shape[0] else moved
 
 
-def exchange_x(spare, main, rest):
+def exchange_x(spare, main, rest, alone):
     places, tall, span = main.shape
     moves = [lambda stack: stack]
     for mask in (1, 2, 3):
         for count in range(1, rest.shape[0] + 1):
             moves.append(functools.partial(move_spare, mask, count))
-    main, rest = lax.optimization_barrier((main, lax.switch(spare, moves, rest)))
+    rest = lax.switch(spare, moves, rest)
+    if alone:
+        main, rest = lax.optimization_barrier((main, rest))
     sent = main.reshape(4, CAP * tall, span)
     main = lax.all_to_all(sent, "wide", 0, 0, axis_index_groups=X_SETS).reshape(places, tall, span)
     return lax.optimization_barrier((main, rest))
@@ -47,13 +49,24 @@
     rest[...] = jnp.zeros_like(rest)
     beyond = jnp.int32(0)
     index = jnp.int32(0)
+    places = []
+    fresh = []
     for r in range(rounds):
-        before = sum([(x_masks[s] == x_masks[r]).astype(jnp.int32) for s in range(r)], jnp.int32(0))
+        twin = jnp.int32(-1)
+        before = jnp.int32(0)
+        for s in range(r):
+            twin = jnp.where((masks[s] >> 1) == (masks[r] >> 1), places[s], twin)
+            before += jnp.where(x_masks[s] == x_masks[r], fresh[s], 0)
+        new = twin < 0
         fits = before < CAP
         place = jnp.where(fits, (my_x ^ x_masks[r]) * CAP + before, MAIN + beyond)
-        beyond += jnp.where(fits, 0, 1)
+        beyond += jnp.where(new & ~fits, 1, 0)
         over = before - CAP + 1
-        index = jnp.where(fits | (x_masks[r] == 0), index, (x_masks[r] - 1) * (rounds - CAP) + over)
+        moves = new & ~fits & (x_masks[r] != 0)
+        index = jnp.where(moves, (x_masks[r] - 1) * (rounds - CAP) + over, index)
+        place = jnp.where(new, place, twin)
+        places.append(place)
+        fresh.append(new.astype(jnp.int32))
         home = my_z ^ (masks[r] >> 3)
         info[r] = masks[r] & 1
         info[rounds + r] = place
@@ -149,11 +162,11 @@
 
             @pl.when(place < MAIN)
             def _():
-                back_main[place, kind_rows, :] = slope
+                back_main[place, kind_rows, :] += slope
 
             @pl.when(place >= MAIN)
             def _():
-                back_rest[place - MAIN, kind_rows, :] = slope
+                back_rest[place - MAIN, kind_rows, :] += slope
 
 
 def local(
@@ -196,7 +209,7 @@
         out_specs=[vmem, vmem, smem, smem, smem],
         compiler_params=pltpu.CompilerParams(vmem_limit_bytes=PICK_VMEM),
     )(partner_table, gathered)
-    main, rest = exchange_x(spare[0], main, rest)
+    main, rest = exchange_x(spare[0], main, rest, False)
     main, rest, own = pl.pallas_call(
         functools.partial(grad_kernel, rounds),
         out_shape=[
@@ -221,7 +234,7 @@
         other_pictures,
         other_texts,
     )
-    main, rest = exchange_x(spare[0], main.astype(jnp.float16), rest.astype(jnp.float16))
+    main, rest = exchange_x(spare[0], main.astype(jnp.float16), rest.astype(jnp.float16), True)
     main, homes = lax.optimization_barrier((main, homes))
 
     def by_home(stack, places):

time: 136 us -> 115 us (0.85)
  the two profiles are of different devices: /device:TPU:64 before, /device:TPU:112 now
where the time goes in v4:
time: 115 us; the launch traced here: 114 us
  blocking collectives  73.5 us (64%)
  waiting for transfers between devices  14.5 us (13%)
  Pallas kernels  8.99 us (8%)
  starting transfers between devices  8.64 us (8%)
  local copies, waits for them, and re-layouts  3.92 us (3%)
  between operations  2.76 us (2%)
  other arithmetic  2.09 us (2%)
    all_gather x1, blocking collectives, local(): gathered = lax.all_gather(shares, 'wide', axis_index_groups=Z_SETS)  31.8 us
    all_to_all x1, blocking collectives, local(): arrived = lax.all_to_all(sums, 'wide', 0, 0, axis_index_groups=Z_SETS)  23.7 us
    all_to_all x1, blocking collectives, exchange_x(): lax.all_to_all(sent, 'wide', 0, 0, axis_index_groups=X_SETS)  18 us
    all_to_all x1, waiting for transfers between devices, exchange_x(): lax.all_to_all(sent, 'wide', 0, 0, axis_index_groups=X_SETS)  14.5 us
    pallas_call x1, Pallas kernels, local(): pl.pallas_call(functools.partial(grad_kernel, rounds), out_shape=[jax.Sha...  6.95 us
    all_to_all x1, starting transfers between devices, exchange_x(): lax.all_to_all(sent, 'wide', 0, 0, axis_index_groups=X_SETS)  4.3 us
    ppermute x1, starting transfers between devices, local(): other_texts = lax.ppermute(sentence_vectors, 'wide', xor_pairs(1))  2.41 us
  transfers between devices with their start and end apart: 3, of which 1 were waited for; matrix products, arithmetic and copies ran while one was open for 1% of the time, Pallas kernels for 2%

profile of v4, /device:TPU:112, one launch (start us, length us, event | category | flops | bytes accessed | tf_op | source)
XLA Modules:
  0.0 114.5 jit_solution(16776556196512884238)
XLA Ops:
  0.6 1.9 %collective-permute-start.18 = (bf16[768,1152]{1,0:T(8,128)(2,1)}, bf16[768,1152]{1,0:T(8,128)(2,1)}, u32[]{:S(2)}, u32[]{:S(2)}) collective-permute-start(bf16[768,1152]{1,0:T(8,128)(2,1)} %pictures.1), channel_id=1, source_target_pairs={{0,24},{24,0},{48,72},{72,48},{96,120},{120,96},{144,168},{168,144... | collective-permute-start | bytes 5308424 | tf_op jit(solution)/shard_map/ppermute | solution.py:187
  2.6 2.4 %collective-permute-start.19 = (bf16[768,1152]{1,0:T(8,128)(2,1)}, bf16[768,1152]{1,0:T(8,128)(2,1)}, u32[]{:S(2)}, u32[]{:S(2)}) collective-permute-start(bf16[768,1152]{1,0:T(8,128)(2,1)} %texts.1), channel_id=1, source_target_pairs={{0,24},{24,0},{48,72},{72,48},{96,120},{120,96},{144,168},{168,144... | collective-permute-start | bytes 5308424 | tf_op jit(solution)/shard_map/ppermute | solution.py:188
  5.0 0.9 constant_dynamic-slice_fusion
  6.0 0.0 copy-start.3
  6.0 31.8 %all-gather = bf16[256,1152]{1,0:T(8,128)(2,1)S(1)} all-gather(bf16[64,1152]{1,0:T(8,128)(2,1)S(1)} %pad_maximum_fusion.12.shares), channel_id=2, replica_groups={{0,192,384,576},{24,216,408,600},{48,240,432,624},{72,264,456,648},{96,..., dimensions={0}, use_global_device_ids=true | all-gather | bytes 737280 | tf_op jit(solution)/shard_map/all_gather | solution.py:196
  37.8 0.0 copy-start.2
  37.8 0.7 copy-done.2
  38.4 2.0 %shard_map.77 = (bf16[8,64,1152]{2,1,0:T(8,128)(2,1)}, bf16[3,64,1152]{2,1,0:T(8,128)(2,1)}, s32[1]{0:T(128)}, s32[10]{0:T(128)S(1)}, s32[11]{0:T(128)S(1)}) custom-call(s32[5,32]{1,0:T(8,128)S(1)} %copy-done.2, bf16[4,64,1152]{2,1,0:T(8,128)(2,1)S(1)} %bitcast.8), custom_call_target="tpu_custom_call" | custom-call | tf_op jit(solution)/shard_map/pallas_call | solution.py:199
  40.5 4.3 %all-to-all-start = ((bf16[4,128,1152]{2,1,0:T(8,128)(2,1)}), bf16[4,128,1152]{2,1,0:T(8,128)(2,1)S(1)}, u32[]{:S(2)}, u32[]{:S(2)}) async-start(bf16[4,128,1152]{2,1,0:T(8,128)(2,1)} %bitcast.1), calls=%async_computation | async-start | bytes 2359296 | tf_op jit(solution)/shard_map/all_to_all | solution.py:37
  46.1 0.0 copy-done.3
  46.8 0.0 copy-start
  46.8 14.5 %all-to-all-done = bf16[4,128,1152]{2,1,0:T(8,128)(2,1)S(1)} async-done(((bf16[4,128,1152]{2,1,0:T(8,128)(2,1)}), bf16[4,128,1152]{2,1,0:T(8,128)(2,1)S(1)}, u32[]{:S(2)}, u32[]{:S(2)}) %all-to-all-start) | async-done | bytes 1179680 | tf_op jit(solution)/shard_map/all_to_all | solution.py:37
  61.3 0.0 collective-permute-done.18.other_pictures
  61.3 0.0 collective-permute-done.19.other_texts
  61.3 0.0 copy-done
  61.3 0.0 copy-start.1
  61.3 1.5 %copy-done.1 = bf16[768,1152]{1,0:T(8,128)(2,1)S(1)} copy-done((bf16[768,1152]{1,0:T(8,128)(2,1)S(1)}, bf16[768,1152]{1,0:T(8,128)(2,1)}, u32[]{:S(2)}) %copy-start.1) | copy-done | bytes 1769496
  62.8 6.9 %shard_map.78 = (f32[8,64,1152]{2,1,0:T(8,128)S(1)}, f32[3,64,1152]{2,1,0:T(8,128)S(1)}, f32[64,1152]{1,0:T(8,128)S(1)}) custom-call(s32[10]{0:T(128)S(1)} %get-tuple-element.62.info, f32[1]{0:T(128)S(6)} %copy.28.steepness, f32[1]{0:T(128)S(6)} %copy.29.shift, s32[1,768]{1,0:T(1,128)S(1)} %broadcast_in_dim.51.matched, ...), custom_call_target="tpu_custom_call" | custom-call | tf_op jit(solution)/shard_map/pallas_call | solution.py:213
  69.8 0.2 convert_element_type.50
  70.0 0.1 convert_element_type.51
  70.1 18.0 %all_to_all.15 = f16[4,128,1152]{2,1,0:T(8,128)(2,1)S(1)} all-to-all(f16[4,128,1152]{2,1,0:T(8,128)(2,1)S(1)} %bitcast.10), channel_id=1, replica_groups={{0,48,96,144},{24,72,120,168},{192,240,288,336},{216,264,312,360},{384,..., dimensions={0} | all-to-all | bytes 2359296 | tf_op jit(solution)/shard_map/all_to_all | solution.py:37
  88.1 0.1 slice.85
  88.2 0.1 convert_element_type.53
  88.2 0.2 convert_element_type.52
  88.4 0.3 select_reduce_fusion.1
  88.7 1.0 select_reduce_fusion
  89.8 0.1 add_convert_fusion
  89.9 23.7 %all_to_all.16 = f16[4,64,1152]{2,1,0:T(8,128)(2,1)S(1)} all-to-all(f16[4,64,1152]{2,1,0:T(8,128)(2,1)S(1)} %add_convert_fusion), channel_id=1, replica_groups={{0,192,384,576},{24,216,408,600},{48,240,432,624},{72,264,456,648},{96,..., dimensions={0} | all-to-all | bytes 1179648 | tf_op jit(solution)/shard_map/all_to_all | solution.py:245
  113.6 0.1 convert_reduce_fusion
  113.8 0.7 fusion
  (7 shorter events, 0.1 us)
Async XLA Ops:
  0.6 60.7 %collective-permute-start.18 = (bf16[768,1152]{1,0:T(8,128)(2,1)}, bf16[768,1152]{1,0:T(8,128)(2,1)}, u32[]{:S(2)}, u32[]{:S(2)}) collective-permute-start(bf16[768,1152]{1,0:T(8,128)(2,1)} %pictures.1), channel_id=1, source_target_pairs={{0,24},{24,0},{48,72},{72,48},{96,120},{120,96},{144,168},{168,144... | collective-permute-start | bytes 5308424 | tf_op jit(solution)/shard_map/ppermute | solution.py:187
  2.6 58.8 %collective-permute-start.19 = (bf16[768,1152]{1,0:T(8,128)(2,1)}, bf16[768,1152]{1,0:T(8,128)(2,1)}, u32[]{:S(2)}, u32[]{:S(2)}) collective-permute-start(bf16[768,1152]{1,0:T(8,128)(2,1)} %texts.1), channel_id=1, source_target_pairs={{0,24},{24,0},{48,72},{72,48},{96,120},{120,96},{144,168},{168,144... | collective-permute-start | bytes 5308424 | tf_op jit(solution)/shard_map/ppermute | solution.py:188
  6.0 40.2 %copy-start.3 = (s32[768]{0:T(1024)S(1)}, s32[768]{0:T(1024)}, u32[]{:S(2)}) copy-start(s32[768]{0:T(1024)} %param.28) | copy-start | bytes 9220
  37.8 0.7 copy-start.2
  40.5 20.8 %all-to-all-start = ((bf16[4,128,1152]{2,1,0:T(8,128)(2,1)}), bf16[4,128,1152]{2,1,0:T(8,128)(2,1)S(1)}, u32[]{:S(2)}, u32[]{:S(2)}) async-start(bf16[4,128,1152]{2,1,0:T(8,128)(2,1)} %bitcast.1), calls=%async_computation | async-start | bytes 2359296 | tf_op jit(solution)/shard_map/all_to_all | solution.py:37
  46.8 14.6 %copy-start = (bf16[768,1152]{1,0:T(8,128)(2,1)S(1)}, bf16[768,1152]{1,0:T(8,128)(2,1)}, u32[]{:S(2)}) copy-start(bf16[768,1152]{1,0:T(8,128)(2,1)} %texts.1) | copy-start | bytes 5308420
  61.3 1.5 %copy-start.1 = (bf16[768,1152]{1,0:T(8,128)(2,1)S(1)}, bf16[768,1152]{1,0:T(8,128)(2,1)}, u32[]{:S(2)}) copy-start(bf16[768,1152]{1,0:T(8,128)(2,1)} %pictures.1) | copy-start | bytes 5308420

commit v5 on v4

--- a/solution.py
+++ b/solution.py
@@ -108,8 +108,16 @@
     back_rest,
     own,
     left,
+    held,
+    sems,
 ):
     rows, span = pictures.shape
+    loads = [
+        pltpu.make_async_copy(source, held.at[k], sems.at[k])
+        for k, source in enumerate([texts, other_texts, pictures, other_pictures])
+    ]
+    for load in loads:
+        load.start()
     share = main.shape[1] // 2
     first = lax.axis_index("wide") * rows
     begin = lax.axis_index("narrow") * share
@@ -136,9 +144,12 @@
             def _():
                 left[kind, left_rows, :] = rest[place - MAIN, kind_rows, :]
 
-    for kind, (block, other) in enumerate([(texts, other_texts), (pictures, other_pictures)]):
+    for kind in range(2):
+        block, other = held.at[2 * kind], held.at[2 * kind + 1]
         kind_rows = slice(kind * share, (kind + 1) * share)
+        loads[2 * kind].wait()
         near = dot_last(left[kind], block[...])
+        loads[2 * kind + 1].wait()
         far = dot_last(left[kind, : rounds * share, :], other[...])
         near_weights = []
         far_weights = []
@@ -217,9 +228,13 @@
             jax.ShapeDtypeStruct(rest_shape, jnp.float32),
             jax.ShapeDtypeStruct((2 * share, span), jnp.float32),
         ],
-        in_specs=[smem, smem, smem] + [vmem] * 8,
+        in_specs=[smem, smem, smem] + [vmem] * 4 + [pl.BlockSpec(memory_space=pltpu.HBM)] * 4,
         out_specs=[vmem, vmem, vmem],
-        scratch_shapes=[pltpu.VMEM((2, (rounds + 1) * share, span), jnp.bfloat16)],
+        scratch_shapes=[
+            pltpu.VMEM((2, (rounds + 1) * share, span), jnp.bfloat16),
+            pltpu.VMEM((4, rows, span), jnp.bfloat16),
+            pltpu.SemaphoreType.DMA((4,)),
+        ],
         compiler_params=pltpu.CompilerParams(vmem_limit_bytes=GRAD_VMEM),
     )(
         info,
@@ -229,10 +244,10 @@
         shares,
         main,
         rest,
-        picture_vectors,
-        sentence_vectors,
-        other_pictures,
-        other_texts,
+        *[
+            pltpu.with_memory_space_constraint(block, pltpu.HBM)
+            for block in (picture_vectors, sentence_vectors, other_pictures, other_texts)
+        ],
     )
     main, rest = exchange_x(spare[0], main.astype(jnp.float16), rest.astype(jnp.float16), True)
     main, homes = lax.optimization_barrier((main, homes))

time: 115 us -> 114 us (level)
  the two profiles are of different devices: /device:TPU:112 before, /device:TPU:136 now
where the time goes in v5:
time: 114 us; the launch traced here: 113 us
  blocking collectives  76 us (67%)
  waiting for transfers between devices  12.1 us (11%)
  Pallas kernels  9.26 us (8%)
  starting transfers between devices  8.64 us (8%)
  between operations  2.74 us (2%)
  local copies, waits for them, and re-layouts  2.44 us (2%)
  other arithmetic  2.09 us (2%)
    all_gather x1, blocking collectives, local(): gathered = lax.all_gather(shares, 'wide', axis_index_groups=Z_SETS)  31.4 us
    all_to_all x1, blocking collectives, local(): arrived = lax.all_to_all(sums, 'wide', 0, 0, axis_index_groups=Z_SETS)  29.3 us
    all_to_all x1, blocking collectives, exchange_x(): lax.all_to_all(sent, 'wide', 0, 0, axis_index_groups=X_SETS)  15.3 us
    all_to_all x1, waiting for transfers between devices, exchange_x(): lax.all_to_all(sent, 'wide', 0, 0, axis_index_groups=X_SETS)  12.1 us
    pallas_call x1, Pallas kernels, local(): pl.pallas_call(functools.partial(grad_kernel, rounds), out_shape=[jax.Sha...  7.36 us
    all_to_all x1, starting transfers between devices, exchange_x(): lax.all_to_all(sent, 'wide', 0, 0, axis_index_groups=X_SETS)  4.3 us
    ppermute x1, starting transfers between devices, local(): other_texts = lax.ppermute(sentence_vectors, 'wide', xor_pairs(1))  2.41 us
  transfers between devices with their start and end apart: 3, of which 1 were waited for; matrix products, arithmetic and copies ran while one was open for 1% of the time, Pallas kernels for 2%

profile of v5, /device:TPU:136, one launch (start us, length us, event | category | flops | bytes accessed | tf_op | source)
XLA Modules:
  0.0 113.3 jit_solution(7243663021175657697)
XLA Ops:
  0.6 1.9 %collective-permute-start.18 = (bf16[768,1152]{1,0:T(8,128)(2,1)}, bf16[768,1152]{1,0:T(8,128)(2,1)}, u32[]{:S(2)}, u32[]{:S(2)}) collective-permute-start(bf16[768,1152]{1,0:T(8,128)(2,1)} %pictures.1), channel_id=1, source_target_pairs={{0,24},{24,0},{48,72},{72,48},{96,120},{120,96},{144,168},{168,144... | collective-permute-start | bytes 5308424 | tf_op jit(solution)/shard_map/ppermute | solution.py:198
  2.6 2.4 %collective-permute-start.19 = (bf16[768,1152]{1,0:T(8,128)(2,1)}, bf16[768,1152]{1,0:T(8,128)(2,1)}, u32[]{:S(2)}, u32[]{:S(2)}) collective-permute-start(bf16[768,1152]{1,0:T(8,128)(2,1)} %texts.1), channel_id=1, source_target_pairs={{0,24},{24,0},{48,72},{72,48},{96,120},{120,96},{144,168},{168,144... | collective-permute-start | bytes 5308424 | tf_op jit(solution)/shard_map/ppermute | solution.py:199
  5.0 0.9 constant_dynamic-slice_fusion
  6.0 0.0 copy-start.1
  6.0 31.4 %all-gather = bf16[256,1152]{1,0:T(8,128)(2,1)S(1)} all-gather(bf16[64,1152]{1,0:T(8,128)(2,1)S(1)} %pad_maximum_fusion.12.shares), channel_id=2, replica_groups={{0,192,384,576},{24,216,408,600},{48,240,432,624},{72,264,456,648},{96,..., dimensions={0}, use_global_device_ids=true | all-gather | bytes 737280 | tf_op jit(solution)/shard_map/all_gather | solution.py:207
  37.3 0.0 copy-start
  37.3 0.7 copy-done
  38.0 1.9 %shard_map.77 = (bf16[8,64,1152]{2,1,0:T(8,128)(2,1)}, bf16[3,64,1152]{2,1,0:T(8,128)(2,1)S(1)}, s32[1]{0:T(128)}, s32[10]{0:T(128)S(1)}, s32[11]{0:T(128)S(1)}) custom-call(s32[5,32]{1,0:T(8,128)S(1)} %copy-done, bf16[4,64,1152]{2,1,0:T(8,128)(2,1)S(1)} %bitcast.8), custom_call_target="tpu_custom_call" | custom-call | tf_op jit(solution)/shard_map/pallas_call | solution.py:210
  39.9 4.3 %all-to-all-start = ((bf16[4,128,1152]{2,1,0:T(8,128)(2,1)}), bf16[4,128,1152]{2,1,0:T(8,128)(2,1)S(1)}, u32[]{:S(2)}, u32[]{:S(2)}) async-start(bf16[4,128,1152]{2,1,0:T(8,128)(2,1)} %bitcast.1), calls=%async_computation | async-start | bytes 2359296 | tf_op jit(solution)/shard_map/all_to_all | solution.py:37
  45.5 0.0 copy-done.1
  46.2 12.1 %all-to-all-done = bf16[4,128,1152]{2,1,0:T(8,128)(2,1)S(1)} async-done(((bf16[4,128,1152]{2,1,0:T(8,128)(2,1)}), bf16[4,128,1152]{2,1,0:T(8,128)(2,1)S(1)}, u32[]{:S(2)}, u32[]{:S(2)}) %all-to-all-start) | async-done | bytes 1179680 | tf_op jit(solution)/shard_map/all_to_all | solution.py:37
  58.3 0.0 collective-permute-done.18.other_pictures
  58.3 0.0 collective-permute-done.19.other_texts
  58.3 7.4 %shard_map.78 = (f32[8,64,1152]{2,1,0:T(8,128)S(1)}, f32[3,64,1152]{2,1,0:T(8,128)S(1)}, f32[64,1152]{1,0:T(8,128)S(1)}) custom-call(s32[10]{0:T(128)S(1)} %get-tuple-element.62.info, f32[1]{0:T(128)S(6)} %copy.28.steepness, f32[1]{0:T(128)S(6)} %copy.29.shift, s32[1,768]{1,0:T(1,128)S(1)} %broadcast_in_dim.51.matched, ...), custom_call_target="tpu_custom_call" | custom-call | tf_op jit(solution)/shard_map/pallas_call | solution.py:224
  65.7 0.2 convert_element_type.50
  65.9 0.1 convert_element_type.51
  66.0 15.3 %all_to_all.15 = f16[4,128,1152]{2,1,0:T(8,128)(2,1)S(1)} all-to-all(f16[4,128,1152]{2,1,0:T(8,128)(2,1)S(1)} %bitcast.10), channel_id=1, replica_groups={{0,48,96,144},{24,72,120,168},{192,240,288,336},{216,264,312,360},{384,..., dimensions={0} | all-to-all | bytes 2359296 | tf_op jit(solution)/shard_map/all_to_all | solution.py:37
  81.3 0.1 slice.85
  81.4 0.1 convert_element_type.53
  81.5 0.2 convert_element_type.52
  81.6 0.3 select_reduce_fusion.1
  82.0 1.0 select_reduce_fusion
  83.0 0.1 add_convert_fusion
  83.2 29.3 %all_to_all.16 = f16[4,64,1152]{2,1,0:T(8,128)(2,1)S(1)} all-to-all(f16[4,64,1152]{2,1,0:T(8,128)(2,1)S(1)} %add_convert_fusion), channel_id=1, replica_groups={{0,192,384,576},{24,216,408,600},{48,240,432,624},{72,264,456,648},{96,..., dimensions={0} | all-to-all | bytes 1179648 | tf_op jit(solution)/shard_map/all_to_all | solution.py:260
  112.5 0.1 convert_reduce_fusion
  112.6 0.7 fusion
  (7 shorter events, 0.1 us)
Async XLA Ops:
  0.6 57.7 %collective-permute-start.18 = (bf16[768,1152]{1,0:T(8,128)(2,1)}, bf16[768,1152]{1,0:T(8,128)(2,1)}, u32[]{:S(2)}, u32[]{:S(2)}) collective-permute-start(bf16[768,1152]{1,0:T(8,128)(2,1)} %pictures.1), channel_id=1, source_target_pairs={{0,24},{24,0},{48,72},{72,48},{96,120},{120,96},{144,168},{168,144... | collective-permute-start | bytes 5308424 | tf_op jit(solution)/shard_map/ppermute | solution.py:198
  2.6 55.8 %collective-permute-start.19 = (bf16[768,1152]{1,0:T(8,128)(2,1)}, bf16[768,1152]{1,0:T(8,128)(2,1)}, u32[]{:S(2)}, u32[]{:S(2)}) collective-permute-start(bf16[768,1152]{1,0:T(8,128)(2,1)} %texts.1), channel_id=1, source_target_pairs={{0,24},{24,0},{48,72},{72,48},{96,120},{120,96},{144,168},{168,144... | collective-permute-start | bytes 5308424 | tf_op jit(solution)/shard_map/ppermute | solution.py:199
  6.0 39.6 %copy-start.1 = (s32[768]{0:T(1024)S(1)}, s32[768]{0:T(1024)}, u32[]{:S(2)}) copy-start(s32[768]{0:T(1024)} %param.28) | copy-start | bytes 9220
  37.3 0.7 copy-start
  39.9 18.4 %all-to-all-start = ((bf16[4,128,1152]{2,1,0:T(8,128)(2,1)}), bf16[4,128,1152]{2,1,0:T(8,128)(2,1)S(1)}, u32[]{:S(2)}, u32[]{:S(2)}) async-start(bf16[4,128,1152]{2,1,0:T(8,128)(2,1)} %bitcast.1), calls=%async_computation | async-start | bytes 2359296 | tf_op jit(solution)/shard_map/all_to_all | solution.py:37

commit v6 on v5

--- a/solution.py
+++ b/solution.py
@@ -38,15 +38,18 @@
     return lax.optimization_barrier((main, rest))
 
 
-def pick_kernel(rounds, table, gathered, main, rest, spare, info, homes):
+def pick_kernel(rounds, partners, gathered, main, rest, spare, info, homes, table, sem):
+    load = pltpu.make_async_copy(partners, table, sem)
+    load.start()
+    main[...] = jnp.zeros_like(main)
+    rest[...] = jnp.zeros_like(rest)
     my_z = lax.axis_index("wide") // 8
     my_x = (lax.axis_index("wide") // 2) % 4
+    load.wait()
     masks = [table[r, 0] & (WIDE - 1) for r in range(rounds)]
     x_masks = [(mask >> 1) & 3 for mask in masks]
     for place in range(MAIN + rounds - CAP):
         homes[place] = -1
-    main[...] = jnp.zeros_like(main)
-    rest[...] = jnp.zeros_like(rest)
     beyond = jnp.int32(0)
     index = jnp.int32(0)
     places = []
@@ -216,10 +219,11 @@
             jax.ShapeDtypeStruct((2 * rounds,), jnp.int32),
             jax.ShapeDtypeStruct((MAIN + rounds - CAP,), jnp.int32),
         ],
-        in_specs=[smem, vmem],
+        in_specs=[pl.BlockSpec(memory_space=pltpu.HBM), vmem],
         out_specs=[vmem, vmem, smem, smem, smem],
+        scratch_shapes=[pltpu.SMEM(partner_table.shape, jnp.int32), pltpu.SemaphoreType.DMA],
         compiler_params=pltpu.CompilerParams(vmem_limit_bytes=PICK_VMEM),
-    )(partner_table, gathered)
+    )(pltpu.with_memory_space_constraint(partner_table, pltpu.HBM), gathered)
     main, rest = exchange_x(spare[0], main, rest, False)
     main, rest, own = pl.pallas_call(
         functools.partial(grad_kernel, rounds),

time: 114 us -> 113 us (level)
  the two profiles are of different devices: /device:TPU:136 before, /device:TPU:96 now
where the time goes in v6:
time: 113 us
  blocking collectives  73.6 us (65%)
  waiting for transfers between devices  14.5 us (13%)
  Pallas kernels  9.23 us (8%)
  starting transfers between devices  8.64 us (8%)
  between operations  2.74 us (2%)
  other arithmetic  2.09 us (2%)
  local copies, waits for them, and re-layouts  1.75 us (2%)
    all_gather x1, blocking collectives, local(): gathered = lax.all_gather(shares, 'wide', axis_index_groups=Z_SETS)  31.8 us
    all_to_all x1, blocking collectives, local(): arrived = lax.all_to_all(sums, 'wide', 0, 0, axis_index_groups=Z_SETS)  23.8 us
    all_to_all x1, blocking collectives, exchange_x(): lax.all_to_all(sent, 'wide', 0, 0, axis_index_groups=X_SETS)  18 us
    all_to_all x1, waiting for transfers between devices, exchange_x(): lax.all_to_all(sent, 'wide', 0, 0, axis_index_groups=X_SETS)  14.5 us
    pallas_call x1, Pallas kernels, local(): pl.pallas_call(functools.partial(grad_kernel, rounds), out_shape=[jax.Sha...  7.34 us
    all_to_all x1, starting transfers between devices, exchange_x(): lax.all_to_all(sent, 'wide', 0, 0, axis_index_groups=X_SETS)  4.3 us
    ppermute x1, starting transfers between devices, local(): other_texts = lax.ppermute(sentence_vectors, 'wide', xor_pairs(1))  2.41 us
  transfers between devices with their start and end apart: 3, of which 1 were waited for; matrix products, arithmetic and copies ran while one was open for 1% of the time, Pallas kernels for 2%

profile of v6, /device:TPU:96, one launch (start us, length us, event | category | flops | bytes accessed | tf_op | source)
XLA Modules:
  0.0 112.6 jit_solution(10799115003015032172)
XLA Ops:
  0.6 1.9 %collective-permute-start.18 = (bf16[768,1152]{1,0:T(8,128)(2,1)}, bf16[768,1152]{1,0:T(8,128)(2,1)}, u32[]{:S(2)}, u32[]{:S(2)}) collective-permute-start(bf16[768,1152]{1,0:T(8,128)(2,1)} %pictures.1), channel_id=1, source_target_pairs={{0,24},{24,0},{48,72},{72,48},{96,120},{120,96},{144,168},{168,144... | collective-permute-start | bytes 5308424 | tf_op jit(solution)/shard_map/ppermute | solution.py:201
  2.6 2.4 %collective-permute-start.19 = (bf16[768,1152]{1,0:T(8,128)(2,1)}, bf16[768,1152]{1,0:T(8,128)(2,1)}, u32[]{:S(2)}, u32[]{:S(2)}) collective-permute-start(bf16[768,1152]{1,0:T(8,128)(2,1)} %texts.1), channel_id=1, source_target_pairs={{0,24},{24,0},{48,72},{72,48},{96,120},{120,96},{144,168},{168,144... | collective-permute-start | bytes 5308424 | tf_op jit(solution)/shard_map/ppermute | solution.py:202
  5.0 0.9 constant_dynamic-slice_fusion
  6.0 0.0 copy-start
  6.0 31.8 %all-gather = bf16[256,1152]{1,0:T(8,128)(2,1)S(1)} all-gather(bf16[64,1152]{1,0:T(8,128)(2,1)S(1)} %pad_maximum_fusion.12.shares), channel_id=2, replica_groups={{0,192,384,576},{24,216,408,600},{48,240,432,624},{72,264,456,648},{96,..., dimensions={0}, use_global_device_ids=true | all-gather | bytes 737280 | tf_op jit(solution)/shard_map/all_gather | solution.py:210
  37.8 1.9 %shard_map.77 = (bf16[8,64,1152]{2,1,0:T(8,128)(2,1)}, bf16[3,64,1152]{2,1,0:T(8,128)(2,1)S(1)}, s32[1]{0:T(128)}, s32[10]{0:T(128)S(1)}, s32[11]{0:T(128)S(1)}) custom-call(s32[5,32]{1,0:T(8,128)} %partners.1, bf16[4,64,1152]{2,1,0:T(8,128)(2,1)S(1)} %bitcast.8), custom_call_target="tpu_custom_call" | custom-call | tf_op jit(solution)/shard_map/pallas_call | solution.py:213
  39.7 4.3 %all-to-all-start = ((bf16[4,128,1152]{2,1,0:T(8,128)(2,1)}), bf16[4,128,1152]{2,1,0:T(8,128)(2,1)S(1)}, u32[]{:S(2)}, u32[]{:S(2)}) async-start(bf16[4,128,1152]{2,1,0:T(8,128)(2,1)} %bitcast.1), calls=%async_computation | async-start | bytes 2359296 | tf_op jit(solution)/shard_map/all_to_all | solution.py:37
  45.3 0.0 copy-done
  46.0 14.5 %all-to-all-done = bf16[4,128,1152]{2,1,0:T(8,128)(2,1)S(1)} async-done(((bf16[4,128,1152]{2,1,0:T(8,128)(2,1)}), bf16[4,128,1152]{2,1,0:T(8,128)(2,1)S(1)}, u32[]{:S(2)}, u32[]{:S(2)}) %all-to-all-start) | async-done | bytes 1179680 | tf_op jit(solution)/shard_map/all_to_all | solution.py:37
  60.5 0.0 collective-permute-done.18.other_pictures
  60.5 0.0 collective-permute-done.19.other_texts
  60.5 7.3 %shard_map.78 = (f32[8,64,1152]{2,1,0:T(8,128)S(1)}, f32[3,64,1152]{2,1,0:T(8,128)S(1)}, f32[64,1152]{1,0:T(8,128)S(1)}) custom-call(s32[10]{0:T(128)S(1)} %get-tuple-element.62.info, f32[1]{0:T(128)S(6)} %copy.28.steepness, f32[1]{0:T(128)S(6)} %copy.29.shift, s32[1,768]{1,0:T(1,128)S(1)} %broadcast_in_dim.51.matched, ...), custom_call_target="tpu_custom_call" | custom-call | tf_op jit(solution)/shard_map/pallas_call | solution.py:228
  67.8 0.2 convert_element_type.50
  68.0 0.1 convert_element_type.51
  68.1 18.0 %all_to_all.15 = f16[4,128,1152]{2,1,0:T(8,128)(2,1)S(1)} all-to-all(f16[4,128,1152]{2,1,0:T(8,128)(2,1)S(1)} %bitcast.10), channel_id=1, replica_groups={{0,48,96,144},{24,72,120,168},{192,240,288,336},{216,264,312,360},{384,..., dimensions={0} | all-to-all | bytes 2359296 | tf_op jit(solution)/shard_map/all_to_all | solution.py:37
  86.2 0.1 slice.85
  86.2 0.1 convert_element_type.53
  86.3 0.2 convert_element_type.52
  86.5 0.3 select_reduce_fusion.1
  86.8 1.0 select_reduce_fusion
  87.8 0.1 add_convert_fusion
  88.0 23.8 %all_to_all.16 = f16[4,64,1152]{2,1,0:T(8,128)(2,1)S(1)} all-to-all(f16[4,64,1152]{2,1,0:T(8,128)(2,1)S(1)} %add_convert_fusion), channel_id=1, replica_groups={{0,192,384,576},{24,216,408,600},{48,240,432,624},{72,264,456,648},{96,..., dimensions={0} | all-to-all | bytes 1179648 | tf_op jit(solution)/shard_map/all_to_all | solution.py:264
  111.7 0.1 convert_reduce_fusion
  111.9 0.7 fusion
  (7 shorter events, 0.1 us)
Async XLA Ops:
  0.6 59.8 %collective-permute-start.18 = (bf16[768,1152]{1,0:T(8,128)(2,1)}, bf16[768,1152]{1,0:T(8,128)(2,1)}, u32[]{:S(2)}, u32[]{:S(2)}) collective-permute-start(bf16[768,1152]{1,0:T(8,128)(2,1)} %pictures.1), channel_id=1, source_target_pairs={{0,24},{24,0},{48,72},{72,48},{96,120},{120,96},{144,168},{168,144... | collective-permute-start | bytes 5308424 | tf_op jit(solution)/shard_map/ppermute | solution.py:201
  2.6 57.9 %collective-permute-start.19 = (bf16[768,1152]{1,0:T(8,128)(2,1)}, bf16[768,1152]{1,0:T(8,128)(2,1)}, u32[]{:S(2)}, u32[]{:S(2)}) collective-permute-start(bf16[768,1152]{1,0:T(8,128)(2,1)} %texts.1), channel_id=1, source_target_pairs={{0,24},{24,0},{48,72},{72,48},{96,120},{120,96},{144,168},{168,144... | collective-permute-start | bytes 5308424 | tf_op jit(solution)/shard_map/ppermute | solution.py:202
  6.0 39.3 %copy-start = (s32[768]{0:T(1024)S(1)}, s32[768]{0:T(1024)}, u32[]{:S(2)}) copy-start(s32[768]{0:T(1024)} %param.28) | copy-start | bytes 9220
  39.7 20.8 %all-to-all-start = ((bf16[4,128,1152]{2,1,0:T(8,128)(2,1)}), bf16[4,128,1152]{2,1,0:T(8,128)(2,1)S(1)}, u32[]{:S(2)}, u32[]{:S(2)}) async-start(bf16[4,128,1152]{2,1,0:T(8,128)(2,1)} %bitcast.1), calls=%async_computation | async-start | bytes 2359296 | tf_op jit(solution)/shard_map/all_to_all | solution.py:37
